TPU v7x, 32 devices: a whole 2x2x4 slice. The times are simulated.
32 devices in a mesh: dp: 4 (over x, core), row: 4 (over z), col: 2 (over y).
Axes of the slice: x: 2, y: 2, z: 4, core: 2. Of those that a mesh axis runs over, the one named last changes fastest.
Arguments:
- activations: float32 [2048, 4096], P('dp', ('row', 'col')), may hold values from -6 to 6
- weight_block: float32 [4096, 15360], P('row', 'col'), may hold values from -0.09375 to 0.09375
- cotangent: float32 [2048, 15360], P(('dp', 'row'), 'col'), may hold values from -6 to 6
Outputs:
- output_act: float32 [2048, 15360], P(('dp', 'row'), 'col')
- input_grad: float32 [2048, 4096], P('dp', ('row', 'col'))
- weight_grad: float32 [4096, 15360], P('row', 'col')
All inputs are finite; a program needn't handle non-finite values.
Results may differ from a plain program's by a relative error of at most 0.000088.
Values sent between devices are 32-bit elements; how exact they have to be, the bound alone decides.
No kernel may reach another device: no remote copies, remote signals or barrier semaphores. Data moves between devices by JAX's collectives and lax.ppermute only.
A program may use at most 256 MiB of HBM per device.

v0:
```python
import jax
import jax.numpy as jnp
from jax import lax
from jax.sharding import PartitionSpec as P


def silu_slope(preact):
    sig = jax.nn.sigmoid(preact)
    return sig * (1.0 + preact * (1.0 - sig))


def body(activations, weight_block, cotangent):
    high = lax.Precision.HIGHEST
    gathered = lax.all_gather(activations, "col", axis=1, tiled=True)
    preact = lax.psum_scatter(
        jnp.dot(gathered, weight_block, precision=high, preferred_element_type=jnp.float32),
        "row",
        scatter_dimension=0,
        tiled=True,
    )
    output_act = jax.nn.silu(preact)
    pre_grad = cotangent * silu_slope(preact)
    all_grads = lax.all_gather(pre_grad, "row", axis=0, tiled=True)
    partial_input = jnp.dot(
        all_grads, weight_block.T, precision=high, preferred_element_type=jnp.float32
    )
    input_grad = lax.psum_scatter(partial_input, "col", scatter_dimension=1, tiled=True)
    local_weight = jnp.dot(
        gathered.T, all_grads, precision=high, preferred_element_type=jnp.float32
    )
    weight_grad = lax.psum(local_weight, "dp")
    return (output_act, input_grad, weight_grad)


def solution(mesh):
    in_specs = (P("dp", ("row", "col")), P("row", "col"), P(("dp", "row"), "col"))
    out_specs = (P(("dp", "row"), "col"), P("dp", ("row", "col")), P("row", "col"))
    return jax.shard_map(body, mesh=mesh, in_specs=in_specs, out_specs=out_specs, check_vma=False)
```

profile of v0, /device:TPU:0, one launch (start us, length us, event | category | flops | bytes accessed | tf_op | source)
XLA Modules:
  0.0 1262.0 jit_solution(12405110686038983324)
XLA Ops:
  7.2 0.0 all-gather.3.cloned.1.call-start
  7.2 0.7 all-gather.3.cloned.1.call-update
  7.9 0.0 reduce-scatter.3.cloned.1.call-start
  7.9 37.4 %all-gather.3.cloned.1.call-done = f32[512,1024]{1,0:T(8,128)} async-done(((f32[512,512]{1,0:T(8,128)}), f32[512,1024]{1,0:T(8,128)}) %all-gather.3.cloned.1.call-update) | async-done | bytes 2097168 | tf_op jit(solution)/shard_map/all_gather | solution.py:14
  45.4 55.9 %fusion.1 = f32[512,7680]{1,0:T(8,128)} fusion(f32[512,1024]{1,0:T(8,128)} %all-gather.3.cloned.1.call-done, f32[1024,7680]{1,0:T(8,128)} %param.4), kind=kOutput, calls=%fused_computation.4 | convolution fusion | flops 48318382080 | bytes 49283072 | tf_op jit(solution)/shard_map/dot_general | solution.py:16
  101.3 0.0 reduce-scatter.3.cloned.1.call-update
  101.3 0.0 all-gather.5.cloned.1.call-start
  101.4 262.7 %reduce-scatter.3.cloned.1.call-done = f32[128,7680]{1,0:T(8,128)} async-done(((f32[512,7680]{1,0:T(8,128)}), f32[128,7680]{1,0:T(8,128)}) %reduce-scatter.3.cloned.1.call-update) | async-done | bytes 3932176 | tf_op jit(solution)/shard_map/reduce_scatter | solution.py:15
  364.1 8.2 multiply_multiply_fusion
  372.2 0.0 copy-start
  372.2 0.0 all-gather.5.cloned.1.call-update
  372.3 0.2 all-reduce.2.cloned.1.call-start
  372.5 270.6 %all-gather.5.cloned.1.call-done = f32[512,7680]{1,0:T(8,128)} async-done(((f32[128,7680]{1,0:T(8,128)}), f32[512,7680]{1,0:T(8,128)}) %all-gather.5.cloned.1.call-update) | async-done | bytes 15728656 | tf_op jit(solution)/shard_map/all_gather | solution.py:23
  643.1 0.0 copy-done
  643.1 54.7 %convolution_bitcast_fusion = f32[1024,7680]{0,1:T(8,128)} fusion(f32[512,7680]{1,0:T(8,128)} %all-gather.5.cloned.1.call-done, f32[512,1024]{1,0:T(8,128)S(1)} %copy-done), kind=kOutput, calls=%fused_computation | convolution fusion | flops 48318382080 | bytes 49283072 | tf_op jit(solution)/shard_map/dot_general | solution.py:28
  697.9 0.0 all-reduce.2.cloned.1.call-update
  697.9 0.3 reduce-scatter.5.cloned.1.call-start
  698.1 56.8 %fusion.2 = f32[512,1024]{1,0:T(8,128)} fusion(f32[512,7680]{1,0:T(8,128)} %all-gather.5.cloned.1.call-done, f32[1024,7680]{1,0:T(8,128)} %param.4), kind=kOutput, calls=%fused_computation.5 | convolution fusion | flops 48318382080 | bytes 49283072 | tf_op jit(solution)/shard_map/dot_general | solution.py:24
  755.0 0.0 reduce-scatter.5.cloned.1.call-update
  755.0 465.5 %all-reduce.2.cloned.1.call-done = f32[1024,7680]{0,1:T(8,128)} async-done(((f32[1024,7680]{0,1:T(8,128)}), f32[1024,7680]{0,1:T(8,128)}) %all-reduce.2.cloned.1.call-update) | async-done | bytes 31457296 | tf_op jit(solution)/shard_map/psum | solution.py:31
  1220.5 30.8 %copy.6 = f32[1024,7680]{1,0:T(8,128)} copy(f32[1024,7680]{0,1:T(8,128)} %all-reduce.2.cloned.1.call-done) | data formatting | bytes 62914560
  1251.4 4.1 reduce-scatter.5.cloned.1.call-done
Async XLA Ops:
  7.2 38.2 %all-gather.3.cloned.1.call-start = ((), (), s32[]{:S(2)}) async-start(), calls=%async_computation.2 | async-start | bytes 3145728 | tf_op jit(solution)/shard_map/all_gather | solution.py:14
  7.9 356.2 %reduce-scatter.3.cloned.1.call-start = ((), (), s32[]{:S(2)}) async-start(), calls=%async_computation.3 | async-start | bytes 19660800 | tf_op jit(solution)/shard_map/reduce_scatter | solution.py:15
  101.3 541.8 %all-gather.5.cloned.1.call-start = ((), (), s32[]{:S(2)}) async-start(), calls=%async_computation.4 | async-start | bytes 19660800 | tf_op jit(solution)/shard_map/all_gather | solution.py:23
  372.2 270.9 %copy-start = (f32[512,1024]{1,0:T(8,128)S(1)}, f32[512,1024]{1,0:T(8,128)}, u32[]{:S(2)}) copy-start(f32[512,1024]{1,0:T(8,128)} %all-gather.3.cloned.1.call-done) | copy-start | bytes 6291460
  372.3 848.2 %all-reduce.2.cloned.1.call-start = ((), (), s32[]{:S(2)}) async-start(), calls=%async_computation.6 | async-start | bytes 62914560 | tf_op jit(solution)/shard_map/psum | solution.py:31
  697.9 557.6 %reduce-scatter.5.cloned.1.call-start = ((), (), s32[]{:S(2)}) async-start(), calls=%async_computation.5 | async-start | bytes 3145728 | tf_op jit(solution)/shard_map/reduce_scatter | solution.py:27
Sparse Core Ops, SparseCore 0:
  9.5 35.8 all-gather.2
  101.4 262.6 reduce-scatter.2
  372.4 270.6 all-gather.4
  698.0 522.4 all-reduce.1
  1223.3 32.1 reduce-scatter.4
where the time goes:
time: 1260 us
  waiting for transfers between devices  1040 us (83%)
  matrix products  167 us (13%)
  local copies, waits for them, and re-layouts  30.9 us (2%)
  between operations  13.8 us (1%)
    psum x1, waiting for transfers between devices, body(): weight_grad = lax.psum(local_weight, 'dp')  466 us
    all_gather x1, waiting for transfers between devices, body(): all_grads = lax.all_gather(pre_grad, 'row', axis=0, tiled=True)  271 us
    reduce_scatter x1, waiting for transfers between devices, body(): lax.psum_scatter(jnp.dot(gathered, weight_block, precision=high, preferre...  263 us
    dot_general x1, matrix products, body(): jnp.dot(all_grads, weight_block.T, precision=high, preferred_element_type...  56.8 us
    dot_general x1, matrix products, body(): jnp.dot(gathered, weight_block, precision=high, preferred_element_type=jn...  55.9 us
    dot_general x1, matrix products, body(): jnp.dot(gathered.T, all_grads, precision=high, preferred_element_type=jnp...  54.7 us
    all_gather x1, waiting for transfers between devices, body(): gathered = lax.all_gather(activations, 'col', axis=1, tiled=True)  37.4 us
    unnamed x3, local copies, waits for them, and re-layouts  30.9 us
  transfers between devices with their start and end apart: 5, of which 5 were waited for; matrix products, arithmetic and copies ran while one was open for 7% of the time, Pallas kernels for 0%

commit v1 on v0

v1 whole, which is shorter than its diff:
```python
import jax
import jax.numpy as jnp
from jax import lax
from jax.experimental import pallas as pl
from jax.experimental.pallas import tpu as pltpu
from jax.sharding import PartitionSpec as P

HIGH = lax.Precision.HIGH
CHUNKS = 6


def mm(lhs, rhs, contract):
    return lax.dot_general(
        lhs, rhs, (contract, ((), ())), precision=HIGH, preferred_element_type=jnp.float32
    )


def widths_of(total, parts):
    unit = 256 if total % 256 == 0 else total // 15
    count = total // unit
    base, extra = divmod(count, parts)
    return [(base + (1 if i < extra else 0)) * unit for i in range(parts)]


def unrotate(blocks, z, n):
    rev = jnp.concatenate([blocks[:1], blocks[1:][::-1]], 0)
    twice = jnp.concatenate([rev, rev], 0)
    return lax.dynamic_slice_in_dim(twice, lax.rem(n - z, n), n, 0)


def tie(value, *others):
    return lax.optimization_barrier((value,) + others)


def place(out, pieces, off, shape):
    half_d, h = pieces[0].shape

    def kernel(*refs):
        src, dst, (held, sem_in, sem_out) = refs[:4], refs[-4], refs[-3:]
        dp = lax.axis_index("dp")
        x, core = dp // 2, dp % 2
        loads, stores = [], []
        for i, (r, c) in enumerate(((core, x), (1 - core, x), (core, 1 - x), (1 - core, 1 - x))):
            rows = pl.ds(pl.multiple_of(r * half_d, 8), half_d)
            cols = pl.ds(pl.multiple_of(off + c * h, 128), h)
            loads.append(pltpu.make_async_copy(src[i], held.at[i], sem_in.at[i]))
            stores.append(pltpu.make_async_copy(held.at[i], dst.at[rows, cols], sem_out.at[i]))
        for load in loads:
            load.start()
        for load, store in zip(loads, stores):
            load.wait()
            store.start()
        for store in stores:
            store.wait()

    args = list(pieces) + ([] if out is None else [out])
    return pl.pallas_call(
        kernel,
        out_shape=jax.ShapeDtypeStruct(shape, jnp.float32),
        in_specs=[pl.BlockSpec(memory_space=pl.ANY)] * len(args),
        out_specs=pl.BlockSpec(memory_space=pl.ANY),
        scratch_shapes=[
            pltpu.VMEM((4, half_d, h), jnp.float32),
            pltpu.SemaphoreType.DMA((4,)),
            pltpu.SemaphoreType.DMA((4,)),
        ],
        compiler_params=pltpu.CompilerParams(vmem_limit_bytes=24 * 2**20),
        input_output_aliases={} if out is None else {4: 0},
        cost_estimate=pl.CostEstimate(flops=0, bytes_accessed=32 * half_d * h, transcendentals=0),
    )(*args)


def make_body(n, ncol):
    swap_x = [(0, 2), (2, 0), (1, 3), (3, 1)]
    swap_core = [(0, 1), (1, 0), (2, 3), (3, 2)]
    swap_y = [(0, 1), (1, 0)]

    def body(act, weight, cot):
        z = lax.axis_index("row")
        dp = lax.axis_index("dp")
        x, core = dp // 2, dp % 2
        y = lax.axis_index("col")
        tokens = act.shape[0]
        tb = tokens // n
        depth = weight.shape[0]
        ff = weight.shape[1]
        half_d = depth // 2

        def gather_y(v):
            if ncol != 2:
                return lax.all_gather(v, "col", axis=1, tiled=True)
            o = lax.ppermute(v, "col", swap_y)
            return jnp.where(y == 0, jnp.concatenate([v, o], 1), jnp.concatenate([o, v], 1))

        own = gather_y(act)
        other = gather_y(lax.ppermute(act, "dp", swap_x))
        both = jnp.stack([own.reshape(n, tb, depth), other.reshape(n, tb, depth)], 1)
        both = jnp.swapaxes(unrotate(both, z, n), 0, 1).reshape(2 * tokens, depth)

        widths = widths_of(ff, CHUNKS)
        offs = [sum(widths[:i]) for i in range(len(widths))]
        up_all = [(i, i + 1) for i in range(n - 1)]

        def up(v, lo, hi):
            return lax.ppermute(v, "row", up_all[lo:hi])

        def down(v, lo, hi):
            return lax.ppermute(v, "row", [(n - 1 - i, n - 1 - j) for i, j in up_all[lo:hi]])

        count = len(widths)
        part, acts, wg, got, ig_terms = {}, {}, {}, {}, []
        out = {}

        def forward(k):
            def run(lhs):
                off, wk = offs[k], widths[k]
                part[k] = mm(lhs, weight[:, off : off + wk], ((1,), (0,))).reshape(n, tb, wk)
                return [part[k]]

            return (lambda: [own]), run

        def weight_product(k):
            def ins():
                ups, dns = got[k]["ups"], got[k]["dns"]
                return [got[k]["g"]] + ups + dns

            def run(g, *recv):
                h = widths[k] // 2
                ups, dns = recv[: n - 1], recv[n - 1 :]
                blocks = [g] + [jnp.where(z > t, ups[t], dns[n - 2 - t]) for t in range(n - 1)]
                gz = jnp.concatenate([v[:, :h] for v in blocks] + [v[:, h:] for v in blocks], 0)
                full = mm(both, gz, ((0,), (0,)))
                keep = lax.dynamic_slice_in_dim(full, core * half_d, half_d, 0)
                give = lax.dynamic_slice_in_dim(full, (1 - core) * half_d, half_d, 0)
                wg[k] = {"gz": gz, "keep": keep, "in": lax.ppermute(give, "dp", swap_core)}
                return [keep]

            return ins, run

        def weight_sum(k):
            def run(keep, recv):
                keep = keep + recv
                wg[k]["keep"] = keep
                if k >= count - 2:
                    wg[k]["x"] = lax.ppermute(keep, "dp", swap_x)
                wg[k]["c"] = lax.ppermute(keep, "dp", swap_core)
                return [keep]

            return (lambda: [wg[k]["keep"], wg[k]["in"]]), run

        def weight_cross(k):
            def run(keep):
                wg[k]["x"] = lax.ppermute(keep, "dp", swap_x)
                return []

            return (lambda: [wg[k]["keep"]]), run

        def weight_back(k):
            def run(v):
                wg[k]["x"] = v
                wg[k]["xc"] = lax.ppermute(v, "dp", swap_core)
                return []

            return (lambda: [wg[k]["x"]]), run

        def weight_place(k):
            def run(*pieces):
                if ff % 256 == 0:
                    out["wg"] = place(out.get("wg"), pieces, offs[k], (depth, ff))
                    return []
                if "wg" not in out:
                    out["wg"] = jnp.zeros((depth, ff), jnp.float32)
                for i, piece in enumerate(pieces):
                    r, c = (core if i in (0, 2) else 1 - core), (x if i < 2 else 1 - x)
                    at = (r * half_d, offs[k] + c * (widths[k] // 2))
                    out["wg"] = lax.dynamic_update_slice(out["wg"], piece, at)
                return []

            return (lambda: [wg[k][i] for i in ("keep", "c", "x", "xc")]), run

        def input_product(k):
            def run(gz):
                h = widths[k] // 2
                wt = lax.dynamic_slice_in_dim(weight, offs[k] + x * h, h, 1)
                term = mm(gz, wt, ((1,), (1,)))
                out["ig"] = term if "ig" not in out else out["ig"] + term
                return [out["ig"]]

            return (lambda: [wg[k]["gz"]]), run

        events = {}
        for k in range(count):
            s, j = k % 2, k // 2
            first = 2 * j * n + s
            end = first + 4 * n - 4
            plan = [(first - 1, forward(k)), (end, weight_product(k)), (end + 1, weight_sum(k))]
            last = k >= count - 2
            cross = end + 1 if last else end + 4 + s
            plan += [] if last else [(cross, weight_cross(k))]
            plan += [(end + (2 if last else 5), input_product(k))]
            plan += [(cross + (1 if last else 3), weight_back(k)), (cross + (2 if last else 4), weight_place(k))]
            for when, what in plan:
                events.setdefault(when, []).append(what)

        done = []

        def half_slot(h, recv):
            nonlocal done
            todo = events.pop(h, [])
            ins = [what[0]() for what in todo]
            flat = tuple(v for group in ins for v in group)
            tied = lax.optimization_barrier(tuple(recv) + tuple(done) + flat)
            new = list(tied[: len(recv)])
            flat = list(tied[len(recv) + len(done) :])
            return new, todo, ins, flat

        def work(todo, ins, flat):
            nonlocal done
            done = []
            for what, group in zip(todo, ins):
                take, flat = flat[: len(group)], flat[len(group) :]
                done += what[1](*take)

        _, todo, ins, flat = half_slot(-1, [])
        work(todo, ins, flat)
        streams = [list(range(s, count, 2)) for s in (0, 1)]
        state = [{"rs": [], "ag": []}, {"rs": [], "ag": []}]
        steps = max(len(v) for v in streams) * n + n - 2
        for h in range(2 * steps):
            s, p = h % 2, h // 2
            st, j, t = state[s], p // n, p % n
            cur = streams[s][j] if j < len(streams[s]) else None
            prev = streams[s][j - 1] if 1 <= j <= len(streams[s]) else None
            same = len(st["rs"]) == 2 and len(st["ag"]) == 2 and st["rs"][0] is st["ag"][0]
            recv = list(st["ag"]) + ([] if same else list(st["rs"]))
            agg = None
            if st["ag"] and prev is not None:
                agg = prev if t < n - 1 else None
            new, todo, ins, flat = [], [], [], []
            if agg is not None:
                got[agg]["ups"].append(st["ag"][0])
                got[agg]["dns"].append(st["ag"][1])
            new, todo, ins, flat = half_slot(h, recv)
            ag = new[:2] if st["ag"] else []
            rs = (ag if same else new[len(ag) :]) if st["rs"] else []
            st["rs"], st["ag"] = [], []
            if t < n - 1:
                has_rs = cur is not None
                has_ag = prev is not None and t < n - 2
                if has_rs:
                    blk_u = lax.dynamic_index_in_dim(part[cur], jnp.clip(z + n - 1 - t, 0, n - 1), 0, keepdims=False)
                    blk_d = lax.dynamic_index_in_dim(part[cur], jnp.clip(z - n + 1 + t, 0, n - 1), 0, keepdims=False)
                merged = has_rs and has_ag and widths[cur] == widths[prev]
                if merged:
                    base = ag if t == 0 else rs
                    su = base[0] + jnp.where(z <= t, blk_u, 0.0)
                    sd = base[1] + jnp.where(n - 1 - z <= t, blk_d, 0.0)
                    st["rs"] = st["ag"] = [up(su, 0, n - 1), down(sd, 0, n - 1)]
                else:
                    if has_rs:
                        su, sd = (blk_u, blk_d) if t == 0 else (rs[0] + blk_u, rs[1] + blk_d)
                        st["rs"] = [up(su, 0, t + 1), down(sd, 0, t + 1)]
                    if has_ag:
                        st["ag"] = [up(ag[0], t + 1, n - 1), down(ag[1], t + 1, n - 1)]
            elif cur is not None:
                pre = lax.dynamic_index_in_dim(part[cur], z, 0, keepdims=False) + rs[0] + rs[1]
                off, wk = offs[cur], widths[cur]
                hw = wk // 2
                sig = jax.nn.sigmoid(pre)
                acts[cur] = pre * sig
                grad = cot[:, off : off + wk] * (sig * (1.0 + pre * (1.0 - sig)))
                left, right = grad[:, :hw], grad[:, hw:]
                mine = jnp.where(x == 0, left, right)
                theirs = jnp.where(x == 0, right, left)
                g = jnp.concatenate([mine, lax.ppermute(theirs, "dp", swap_x)], 1)
                got[cur] = {"g": g, "ups": [], "dns": []}
                st["ag"] = [up(g, 0, n - 1), down(g, 0, n - 1)]
            work(todo, ins, flat)
        for s in (0, 1):
            if state[s]["ag"]:
                got[streams[s][-1]]["ups"].append(state[s]["ag"][0])
                got[streams[s][-1]]["dns"].append(state[s]["ag"][1])
        for h in sorted(events):
            _, todo, ins, flat = half_slot(h, [])
            work(todo, ins, flat)
        ig, wg_out = out["ig"], out["wg"]
        acts = [acts[k] for k in range(count)]

        ig = ig.reshape(2, n, tb, depth)
        mine = ig[0] + lax.ppermute(ig[1], "dp", swap_x)
        if ncol != 2:
            mine = lax.psum_scatter(mine, "col", scatter_dimension=2, tiled=True)
        else:
            keep = lax.dynamic_slice_in_dim(mine, y * half_d, half_d, 2)
            give = lax.dynamic_slice_in_dim(mine, (1 - y) * half_d, half_d, 2)
            mine = keep + lax.ppermute(give, "col", swap_y)
        input_grad = unrotate(mine, z, n).reshape(tokens, -1)
        return jnp.concatenate(acts, 1), input_grad, wg_out

    return body


def solution(mesh):
    in_specs = (P("dp", ("row", "col")), P("row", "col"), P(("dp", "row"), "col"))
    out_specs = (P(("dp", "row"), "col"), P("dp", ("row", "col")), P("row", "col"))
    body = make_body(mesh.shape["row"], mesh.shape["col"])
    return jax.shard_map(body, mesh=mesh, in_specs=in_specs, out_specs=out_specs, check_vma=False)
```

time: 1260 us -> 738 us (0.59)
  waiting for transfers between devices: 1040 us -> 302 us
  starting transfers between devices: 0.6 us -> 190 us
  other arithmetic: 8.17 us -> 59 us
  matrix products: 167 us -> 126 us
  Pallas kernels: 0 us -> 21.8 us
    psum x1 -> x0, waiting for transfers between devices: 466 us -> none  [body(): weight_grad = lax.psum(local_weight, 'dp')]
    all_gather x2 -> x0, waiting for transfers between devices: 308 us -> none  [the longest x1 271 us: body(): all_grads = lax.all_gather(pre_grad, 'row', axis=0, tiled=True)]
    ppermute x0 -> x91, waiting for transfers between devices: none -> 302 us  [the longest x28 143 us: down(): lax.ppermute(v, 'row', [(n - 1 - i, n - 1 - j) for i, j in up_all[lo:hi]])]
    reduce_scatter x2 -> x0, waiting for transfers between devices: 267 us -> none  [the longest x1 263 us: body(): lax.psum_scatter(jnp.dot(gathered, weight_block, precision=high, preferre...]
    ppermute x0 -> x91, starting transfers between devices: none -> 190 us  [the longest x28 124 us: up(): return lax.ppermute(v, 'row', up_all[lo:hi])]
    dot_general x3 -> x18, matrix products: 167 us -> 126 us  [mm(): lax.dot_general(lhs, rhs, (contract, ((), ())), precision=HIGH, preferred...]
    add x0 -> x24, other arithmetic: none -> 22.9 us  [the longest x8 11.5 us: body(): su, sd = (blk_u, blk_d) if t == 0 else (rs[0] + blk_u, rs[1] + blk_d)]
    pallas_call x0 -> x6, Pallas kernels: none -> 21.8 us  [place(): pl.pallas_call(kernel, out_shape=jax.ShapeDtypeStruct(shape, jnp.float32)...]
  transfers between devices with their start and end apart: 5 -> 91, of which waited for: 5 -> 44; matrix products, arithmetic and copies ran while one was open for 7% -> 22% of each run, Pallas kernels for 0% -> 3%
where the time goes in v1:
time: 738 us; the launch traced here: 727 us
  waiting for transfers between devices  302 us (41%)
  starting transfers between devices  190 us (26%)
  matrix products  126 us (17%)
  other arithmetic  59 us (8%)
  local copies, waits for them, and re-layouts  25.4 us (3%)
  Pallas kernels  21.8 us (3%)
    ppermute x28, waiting for transfers between devices, down(): lax.ppermute(v, 'row', [(n - 1 - i, n - 1 - j) for i, j in up_all[lo:hi]])  143 us
    dot_general x18, matrix products, mm(): lax.dot_general(lhs, rhs, (contract, ((), ())), precision=HIGH, preferred...  126 us
    ppermute x28, starting transfers between devices, up(): return lax.ppermute(v, 'row', up_all[lo:hi])  124 us
    ppermute x1, waiting for transfers between devices, body(): mine = ig[0] + lax.ppermute(ig[1], 'dp', swap_x)  40.7 us
    ppermute x6, waiting for transfers between devices, run(): wg[k]['x'] = lax.ppermute(keep, 'dp', swap_x)  39.3 us
    ppermute x28, starting transfers between devices, down(): lax.ppermute(v, 'row', [(n - 1 - i, n - 1 - j) for i, j in up_all[lo:hi]])  37.5 us
    ppermute x28, waiting for transfers between devices, up(): return lax.ppermute(v, 'row', up_all[lo:hi])  35.4 us
    ppermute x2, waiting for transfers between devices, gather_y(): o = lax.ppermute(v, 'col', swap_y)  23.4 us
  transfers between devices with their start and end apart: 91, of which 44 were waited for; matrix products, arithmetic and copies ran while one was open for 22% of the time, Pallas kernels for 3%

profile of v1, /device:TPU:0, one launch (start us, length us, event | category | flops | bytes accessed | tf_op | source)
XLA Modules:
  0.0 727.5 jit_solution(17138024991612871099)
XLA Ops:
  3.7 23.4 %collective-permute-done = f32[512,512]{1,0:T(8,128)S(1)} collective-permute-done((f32[512,512]{1,0:T(8,128)}, f32[512,512]{1,0:T(8,128)S(1)}, u32[]{:S(2)}, u32[]{:S(2)}) %collective-permute-start) | collective-permute-done | bytes 1048608 | tf_op jit(solution)/shard_map/ppermute | solution.py:92
  29.4 7.7 %fusion.10 = f32[512,1280]{1,0:T(8,128)S(1)} fusion(f32[512,1024]{1,0:T(8,128)S(1)} %maximum_select_fusion, f32[1024,7680]{1,0:T(8,128)} %param.4), kind=kOutput, calls=%fused_computation.14 | convolution fusion | flops 4026531840 | bytes 9961472 | tf_op jit(solution)/shard_map/dot_general | solution.py:13
  43.4 6.9 fusion.8
  147.1 6.9 fusion.6
  187.8 6.9 fusion.4
  225.2 11.7 %collective-permute-done.28 = f32[128,1280]{1,0:T(8,128)S(1)} collective-permute-done((f32[128,1280]{1,0:T(8,128)S(1)}, f32[128,1280]{1,0:T(8,128)S(1)}, u32[]{:S(2)}, u32[]{:S(2)}) %collective-permute-start.28) | collective-permute-done | bytes 655392 | tf_op jit(solution)/shard_map/ppermute | solution.py:108
  257.4 7.4 %collective-permute-done.21 = f32[128,1280]{1,0:T(8,128)S(1)} collective-permute-done((f32[128,1280]{1,0:T(8,128)S(1)}, f32[128,1280]{1,0:T(8,128)S(1)}, u32[]{:S(2)}, u32[]{:S(2)}) %collective-permute-start.21) | collective-permute-done | bytes 655392 | tf_op jit(solution)/shard_map/ppermute | solution.py:108
  266.4 12.3 %collective-permute-done.34 = f32[128,1280]{1,0:T(8,128)S(1)} collective-permute-done((f32[128,1280]{1,0:T(8,128)S(1)}, f32[128,1280]{1,0:T(8,128)S(1)}, u32[]{:S(2)}, u32[]{:S(2)}) %collective-permute-start.34) | collective-permute-done | bytes 655392 | tf_op jit(solution)/shard_map/ppermute | solution.py:108
  285.7 8.8 %collective-permute-done.35 = f32[128,640]{1,0:T(8,128)} collective-permute-done((f32[128,640]{1,0:T(8,128)}, f32[128,640]{1,0:T(8,128)}, u32[]{:S(2)}, u32[]{:S(2)}) %collective-permute-start.35) | collective-permute-done | bytes 327712 | tf_op jit(solution)/shard_map/ppermute | solution.py:275
  302.2 6.9 fusion.2
  344.3 8.4 %fusion.27 = f32[1024,1024]{1,0:T(8,128)} fusion(f32[1024,1024]{1,0:T(8,128)S(1)} %fusion.25, f32[1024,640]{1,0:T(8,128)S(1)} %copy-done.44, f32[1024,7680]{1,0:T(8,128)} %param.4, s32[]{:T(128)S(6)} %select_n.446), kind=kOutput, calls=%fused_computation.39 | convolution fusion | flops 4027580416 | bytes 13631492 | tf_op jit(solution)/shard_map/dot_general | solution.py:13
  364.3 11.4 %collective-permute-done.44 = f32[128,1280]{1,0:T(8,128)S(1)} collective-permute-done((f32[128,1280]{1,0:T(8,128)S(1)}, f32[128,1280]{1,0:T(8,128)S(1)}, u32[]{:S(2)}, u32[]{:S(2)}) %collective-permute-start.44) | collective-permute-done | bytes 655392 | tf_op jit(solution)/shard_map/ppermute | solution.py:108
  393.7 12.4 %collective-permute-done.53 = f32[128,1280]{1,0:T(8,128)S(1)} collective-permute-done((f32[128,1280]{1,0:T(8,128)S(1)}, f32[128,1280]{1,0:T(8,128)S(1)}, u32[]{:S(2)}, u32[]{:S(2)}) %collective-permute-start.53) | collective-permute-done | bytes 655392 | tf_op jit(solution)/shard_map/ppermute | solution.py:108
  422.3 12.1 %collective-permute-done.51 = f32[128,1280]{1,0:T(8,128)S(1)} collective-permute-done((f32[128,1280]{1,0:T(8,128)S(1)}, f32[128,1280]{1,0:T(8,128)S(1)}, u32[]{:S(2)}, u32[]{:S(2)}) %collective-permute-start.51) | collective-permute-done | bytes 655392 | tf_op jit(solution)/shard_map/ppermute | solution.py:108
  455.7 8.3 %collective-permute-done.64 = f32[128,640]{1,0:T(8,128)S(1)} collective-permute-done((f32[128,640]{1,0:T(8,128)S(1)}, f32[128,640]{1,0:T(8,128)S(1)}, u32[]{:S(2)}, u32[]{:S(2)}) %collective-permute-start.64) | collective-permute-done | bytes 327712 | tf_op jit(solution)/shard_map/ppermute | solution.py:275
  488.9 9.3 %collective-permute-done.63 = f32[128,1280]{1,0:T(8,128)} collective-permute-done((f32[128,1280]{1,0:T(8,128)S(1)}, f32[128,1280]{1,0:T(8,128)}, u32[]{:S(2)}, u32[]{:S(2)}) %collective-permute-start.63) | collective-permute-done | bytes 655392 | tf_op jit(solution)/shard_map/ppermute | solution.py:108
  500.4 9.1 %fusion.30 = f32[1024,1024]{1,0:T(8,128)S(1)} fusion(f32[1024,1024]{1,0:T(8,128)} %fusion.27, f32[1024,640]{1,0:T(8,128)} %copy-done.45, f32[1024,7680]{1,0:T(8,128)} %param.4, s32[]{:T(128)S(6)} %select_n.459), kind=kOutput, calls=%fused_computation.40 | convolution fusion | flops 4027580416 | bytes 13631492 | tf_op jit(solution)/shard_map/dot_general | solution.py:13
  511.5 8.4 %fusion.33 = f32[1024,1024]{1,0:T(8,128)} fusion(f32[1024,1024]{1,0:T(8,128)S(1)} %fusion.30, f32[1024,640]{1,0:T(8,128)S(1)} %copy-done.47, f32[1024,7680]{1,0:T(8,128)} %param.4, s32[]{:T(128)S(6)} %select_n.462), kind=kOutput, calls=%fused_computation.41 | convolution fusion | flops 4027580416 | bytes 13631492 | tf_op jit(solution)/shard_map/dot_general | solution.py:13
  523.8 19.9 %collective-permute-done.76 = f32[128,1280]{1,0:T(8,128)S(1)} collective-permute-done((f32[128,1280]{1,0:T(8,128)}, f32[128,1280]{1,0:T(8,128)S(1)}, u32[]{:S(2)}, u32[]{:S(2)}) %collective-permute-start.76) | collective-permute-done | bytes 655392 | tf_op jit(solution)/shard_map/ppermute | solution.py:108
  559.7 16.7 %collective-permute-done.79 = f32[128,1280]{1,0:T(8,128)S(1)} collective-permute-done((f32[128,1280]{1,0:T(8,128)S(1)}, f32[128,1280]{1,0:T(8,128)S(1)}, u32[]{:S(2)}, u32[]{:S(2)}) %collective-permute-start.79) | collective-permute-done | bytes 655392 | tf_op jit(solution)/shard_map/ppermute | solution.py:108
  588.5 19.8 %collective-permute-done.82.refs_2_ = f32[512,640]{1,0:T(8,128)} collective-permute-done((f32[512,640]{1,0:T(8,128)}, f32[512,640]{1,0:T(8,128)}, u32[]{:S(2)}, u32[]{:S(2)}) %collective-permute-start.82) | collective-permute-done | bytes 1310752 | tf_op jit(solution)/shard_map/ppermute | solution.py:145
  612.2 9.4 %fusion.36 = f32[1024,1024]{1,0:T(8,128)S(1)} fusion(f32[1024,1024]{1,0:T(8,128)} %fusion.33, f32[1024,640]{1,0:T(8,128)} %copy-done.42, f32[1024,7680]{1,0:T(8,128)} %param.4, s32[]{:T(128)S(6)} %select_n.469), kind=kOutput, calls=%fused_computation.42 | convolution fusion | flops 4027580416 | bytes 13631492 | tf_op jit(solution)/shard_map/dot_general | solution.py:13
  621.6 18.9 %collective-permute-done.86.refs_2_ = f32[512,640]{1,0:T(8,128)} collective-permute-done((f32[512,640]{1,0:T(8,128)}, f32[512,640]{1,0:T(8,128)}, u32[]{:S(2)}, u32[]{:S(2)}) %collective-permute-start.86) | collective-permute-done | bytes 1310752 | tf_op jit(solution)/shard_map/ppermute | solution.py:145
  655.0 40.7 %collective-permute-done.87 = f32[4,128,1024]{2,1,0:T(8,128)} collective-permute-done((f32[4,128,1024]{2,1,0:T(8,128)}, f32[4,128,1024]{2,1,0:T(8,128)}, u32[]{:S(2)}, u32[]{:S(2)}) %collective-permute-start.87) | collective-permute-done | bytes 2097184 | tf_op jit(solution)/shard_map/ppermute | solution.py:290
  (435 shorter events, 420.8 us)
Async XLA Ops:
  80.3 29.0 %collective-permute-start.29 = (f32[512,512]{1,0:T(8,128)S(1)}, f32[512,512]{1,0:T(8,128)}, u32[]{:S(2)}, u32[]{:S(2)}) collective-permute-start(f32[512,512]{1,0:T(8,128)S(1)} %copy-done.35), channel_id=1, source_target_pairs={{0,16},{16,0},{8,24},{24,8},{1,17},{17,1},{9,25},{25,9},{2,18},{18... | collective-permute-start | bytes 3145736 | tf_op jit(solution)/shard_map/ppermute | solution.py:96
  145.6 27.2 %collective-permute-start.22 = (f32[128,640]{1,0:T(8,128)}, f32[128,640]{1,0:T(8,128)}, u32[]{:S(2)}, u32[]{:S(2)}) collective-permute-start(f32[128,640]{1,0:T(8,128)} %get-tuple-element.382), channel_id=1, source_target_pairs={{0,16},{16,0},{8,24},{24,8},{1,17},{17,1},{9,25},{25,9},{2,18},{18... | collective-permute-start | bytes 983048 | tf_op jit(solution)/shard_map/ppermute | solution.py:275
  251.4 27.3 %collective-permute-start.34 = (f32[128,1280]{1,0:T(8,128)S(1)}, f32[128,1280]{1,0:T(8,128)S(1)}, u32[]{:S(2)}, u32[]{:S(2)}) collective-permute-start(f32[128,1280]{1,0:T(8,128)S(1)} %get-tuple-element.345), channel_id=1, source_target_pairs={{6,4},{4,2},{2,0},{7,5},{5,3},{3,1},{14,12},{12,10},{10,8},{15,13}... | collective-permute-start | bytes 1966088 | tf_op jit(solution)/shard_map/ppermute | solution.py:108
  252.7 27.2 %collective-permute-start.33 = (f32[128,1280]{1,0:T(8,128)S(1)}, f32[128,1280]{1,0:T(8,128)S(1)}, u32[]{:S(2)}, u32[]{:S(2)}) collective-permute-start(f32[128,1280]{1,0:T(8,128)S(1)} %get-tuple-element.346), channel_id=1, source_target_pairs={{0,2},{2,4},{4,6},{1,3},{3,5},{5,7},{8,10},{10,12},{12,14},{9,11},... | collective-permute-start | bytes 1966088 | tf_op jit(solution)/shard_map/ppermute | solution.py:105
  315.3 28.9 %collective-permute-start.39 = (f32[128,1280]{1,0:T(8,128)S(1)}, f32[128,1280]{1,0:T(8,128)S(1)}, u32[]{:S(2)}, u32[]{:S(2)}) collective-permute-start(f32[128,1280]{1,0:T(8,128)S(1)} %get-tuple-element.343), channel_id=1, source_target_pairs={{6,4},{4,2},{2,0},{7,5},{5,3},{3,1},{14,12},{12,10},{10,8},{15,13}... | collective-permute-start | bytes 1966088 | tf_op jit(solution)/shard_map/ppermute | solution.py:108
  316.6 27.7 %collective-permute-start.38 = (f32[128,1280]{1,0:T(8,128)S(1)}, f32[128,1280]{1,0:T(8,128)S(1)}, u32[]{:S(2)}, u32[]{:S(2)}) collective-permute-start(f32[128,1280]{1,0:T(8,128)S(1)} %get-tuple-element.344), channel_id=1, source_target_pairs={{0,2},{2,4},{4,6},{1,3},{3,5},{5,7},{8,10},{10,12},{12,14},{9,11},... | collective-permute-start | bytes 1966088 | tf_op jit(solution)/shard_map/ppermute | solution.py:105
  321.5 34.2 %collective-permute-start.48 = (f32[512,640]{1,0:T(8,128)S(1)}, f32[512,640]{1,0:T(8,128)S(1)}, u32[]{:S(2)}, u32[]{:S(2)}) collective-permute-start(f32[512,640]{1,0:T(8,128)S(1)} %add.419.refs_0_), channel_id=1, source_target_pairs={{0,16},{16,0},{8,24},{24,8},{1,17},{17,1},{9,25},{25,9},{2,18},{18... | collective-permute-start | bytes 3932168 | tf_op jit(solution)/shard_map/ppermute | solution.py:153
  362.7 31.0 %collective-permute-start.54 = (f32[512,640]{1,0:T(8,128)S(1)}, f32[512,640]{1,0:T(8,128)S(1)}, u32[]{:S(2)}, u32[]{:S(2)}) collective-permute-start(f32[512,640]{1,0:T(8,128)S(1)} %add.425.refs_0_), channel_id=1, source_target_pairs={{0,16},{16,0},{8,24},{24,8},{1,17},{17,1},{9,25},{25,9},{2,18},{18... | collective-permute-start | bytes 3932168 | tf_op jit(solution)/shard_map/ppermute | solution.py:153
  392.9 28.1 %collective-permute-start.56 = (f32[512,640]{1,0:T(8,128)S(1)}, f32[512,640]{1,0:T(8,128)S(1)}, u32[]{:S(2)}, u32[]{:S(2)}) collective-permute-start(f32[512,640]{1,0:T(8,128)S(1)} %add.425.refs_0_), channel_id=1, source_target_pairs={{0,8},{8,0},{16,24},{24,16},{1,9},{9,1},{17,25},{25,17},{2,10},{10... | collective-permute-start | bytes 3932168 | tf_op jit(solution)/shard_map/ppermute | solution.py:146
  407.3 32.3 %collective-permute-start.57 = (f32[512,640]{1,0:T(8,128)S(1)}, f32[512,640]{1,0:T(8,128)S(1)}, u32[]{:S(2)}, u32[]{:S(2)}) collective-permute-start(f32[512,640]{1,0:T(8,128)S(1)} %collective-permute-done.54.refs_2_), channel_id=1, source_target_pairs={{0,8},{8,0},{16,24},{24,16},{1,9},{9,1},{17,25},{25,17},{2,10},{10... | collective-permute-start | bytes 3932168 | tf_op jit(solution)/shard_map/ppermute | solution.py:161
  421.0 26.8 %collective-permute-start.60 = (f32[128,1280]{1,0:T(8,128)S(1)}, f32[128,1280]{1,0:T(8,128)S(1)}, u32[]{:S(2)}, u32[]{:S(2)}) collective-permute-start(f32[128,1280]{1,0:T(8,128)S(1)} %get-tuple-element.329), channel_id=1, source_target_pairs={{6,4},{4,2},{2,0},{7,5},{5,3},{3,1},{14,12},{12,10},{10,8},{15,13}... | collective-permute-start | bytes 1966088 | tf_op jit(solution)/shard_map/ppermute | solution.py:108
  471.3 26.9 %collective-permute-start.63 = (f32[128,1280]{1,0:T(8,128)S(1)}, f32[128,1280]{1,0:T(8,128)}, u32[]{:S(2)}, u32[]{:S(2)}) collective-permute-start(f32[128,1280]{1,0:T(8,128)S(1)} %pad_maximum_fusion.6), channel_id=1, source_target_pairs={{6,4},{4,2},{2,0},{7,5},{5,3},{3,1},{14,12},{12,10},{10,8},{15,13}... | collective-permute-start | bytes 1966088 | tf_op jit(solution)/shard_map/ppermute | solution.py:108
  484.5 35.4 %collective-permute-start.73 = (f32[512,640]{1,0:T(8,128)}, f32[512,640]{1,0:T(8,128)}, u32[]{:S(2)}, u32[]{:S(2)}) collective-permute-start(f32[512,640]{1,0:T(8,128)} %add.444.refs_0_), channel_id=1, source_target_pairs={{0,16},{16,0},{8,24},{24,8},{1,17},{17,1},{9,25},{25,9},{2,18},{18... | collective-permute-start | bytes 3932168 | tf_op jit(solution)/shard_map/ppermute | solution.py:153
  522.2 37.4 %collective-permute-start.69 = (f32[512,640]{1,0:T(8,128)S(1)}, f32[512,640]{1,0:T(8,128)S(1)}, u32[]{:S(2)}, u32[]{:S(2)}) collective-permute-start(f32[512,640]{1,0:T(8,128)S(1)} %copy-done), channel_id=1, source_target_pairs={{0,16},{16,0},{8,24},{24,8},{1,17},{17,1},{9,25},{25,9},{2,18},{18... | collective-permute-start | bytes 3932168 | tf_op jit(solution)/shard_map/ppermute | solution.py:153
  559.1 28.3 %collective-permute-start.80 = (f32[512,640]{1,0:T(8,128)S(1)}, f32[512,640]{1,0:T(8,128)S(1)}, u32[]{:S(2)}, u32[]{:S(2)}) collective-permute-start(f32[512,640]{1,0:T(8,128)S(1)} %copy-done), channel_id=1, source_target_pairs={{0,8},{8,0},{16,24},{24,16},{1,9},{9,1},{17,25},{25,17},{2,10},{10... | collective-permute-start | bytes 3932168 | tf_op jit(solution)/shard_map/ppermute | solution.py:146
  577.6 30.7 %collective-permute-start.82 = (f32[512,640]{1,0:T(8,128)}, f32[512,640]{1,0:T(8,128)}, u32[]{:S(2)}, u32[]{:S(2)}) collective-permute-start(f32[512,640]{1,0:T(8,128)} %add.460.refs_0_), channel_id=1, source_target_pairs={{0,16},{16,0},{8,24},{24,8},{1,17},{17,1},{9,25},{25,9},{2,18},{18... | collective-permute-start | bytes 3932168 | tf_op jit(solution)/shard_map/ppermute | solution.py:145
  579.2 29.2 %collective-permute-start.81 = (f32[512,640]{1,0:T(8,128)S(1)}, f32[512,640]{1,0:T(8,128)S(1)}, u32[]{:S(2)}, u32[]{:S(2)}) collective-permute-start(f32[512,640]{1,0:T(8,128)S(1)} %collective-permute-done.69.refs_2_), channel_id=1, source_target_pairs={{0,8},{8,0},{16,24},{24,16},{1,9},{9,1},{17,25},{25,17},{2,10},{10... | collective-permute-start | bytes 3932168 | tf_op jit(solution)/shard_map/ppermute | solution.py:161
  587.3 34.3 %collective-permute-start.84 = (f32[512,640]{1,0:T(8,128)}, f32[512,640]{1,0:T(8,128)}, u32[]{:S(2)}, u32[]{:S(2)}) collective-permute-start(f32[512,640]{1,0:T(8,128)} %add.460.refs_0_), channel_id=1, source_target_pairs={{0,8},{8,0},{16,24},{24,16},{1,9},{9,1},{17,25},{25,17},{2,10},{10... | collective-permute-start | bytes 3932168 | tf_op jit(solution)/shard_map/ppermute | solution.py:146
  610.7 29.8 %collective-permute-start.86 = (f32[512,640]{1,0:T(8,128)}, f32[512,640]{1,0:T(8,128)}, u32[]{:S(2)}, u32[]{:S(2)}) collective-permute-start(f32[512,640]{1,0:T(8,128)} %add.463.refs_0_), channel_id=1, source_target_pairs={{0,16},{16,0},{8,24},{24,8},{1,17},{17,1},{9,25},{25,9},{2,18},{18... | collective-permute-start | bytes 3932168 | tf_op jit(solution)/shard_map/ppermute | solution.py:145
  612.2 28.3 %collective-permute-start.85 = (f32[512,640]{1,0:T(8,128)}, f32[512,640]{1,0:T(8,128)}, u32[]{:S(2)}, u32[]{:S(2)}) collective-permute-start(f32[512,640]{1,0:T(8,128)} %collective-permute-done.82.refs_2_), channel_id=1, source_target_pairs={{0,8},{8,0},{16,24},{24,16},{1,9},{9,1},{17,25},{25,17},{2,10},{10... | collective-permute-start | bytes 3932168 | tf_op jit(solution)/shard_map/ppermute | solution.py:161
  649.9 45.7 %collective-permute-start.87 = (f32[4,128,1024]{2,1,0:T(8,128)}, f32[4,128,1024]{2,1,0:T(8,128)}, u32[]{:S(2)}, u32[]{:S(2)}) collective-permute-start(f32[4,128,1024]{2,1,0:T(8,128)} %bitcast.56), channel_id=1, source_target_pairs={{0,16},{16,0},{8,24},{24,8},{1,17},{17,1},{9,25},{25,9},{2,18},{18... | collective-permute-start | bytes 6291464 | tf_op jit(solution)/shard_map/ppermute | solution.py:290
  654.4 67.5 %collective-permute-start.89 = (f32[512,640]{1,0:T(8,128)}, f32[512,640]{1,0:T(8,128)S(1)}, u32[]{:S(2)}, u32[]{:S(2)}) collective-permute-start(f32[512,640]{1,0:T(8,128)} %add.463.refs_0_), channel_id=1, source_target_pairs={{0,8},{8,0},{16,24},{24,16},{1,9},{9,1},{17,25},{25,17},{2,10},{10... | collective-permute-start | bytes 3932168 | tf_op jit(solution)/shard_map/ppermute | solution.py:146
  654.5 67.4 %collective-permute-start.90 = (f32[512,640]{1,0:T(8,128)}, f32[512,640]{1,0:T(8,128)S(1)}, u32[]{:S(2)}, u32[]{:S(2)}) collective-permute-start(f32[512,640]{1,0:T(8,128)} %collective-permute-done.86.refs_2_), channel_id=1, source_target_pairs={{0,8},{8,0},{16,24},{24,16},{1,9},{9,1},{17,25},{25,17},{2,10},{10... | collective-permute-start | bytes 3932168 | tf_op jit(solution)/shard_map/ppermute | solution.py:161
  697.9 27.7 %collective-permute-start.88 = (f32[4,128,512]{2,1,0:T(8,128)S(1)}, f32[4,128,512]{2,1,0:T(8,128)S(1)}, u32[]{:S(2)}, u32[]{:S(2)}) collective-permute-start(f32[4,128,512]{2,1,0:T(8,128)S(1)} %constant_dynamic-slice_fusion), channel_id=1, source_target_pairs={{0,1},{1,0},{2,3},{3,2},{4,5},{5,4},{6,7},{7,6},{8,9},{9,8},{10,11... | collective-permute-start | bytes 3145736 | tf_op jit(solution)/shard_map/ppermute | solution.py:296
  (128 other events, 2139.1 us)

commit v2 on v1

--- a/solution.py
+++ b/solution.py
@@ -6,7 +6,7 @@
 from jax.sharding import PartitionSpec as P
 
 HIGH = lax.Precision.HIGH
-CHUNKS = 6
+CHUNKS = 8
 
 
 def mm(lhs, rhs, contract):
@@ -16,7 +16,7 @@
 
 
 def widths_of(total, parts):
-    unit = 256 if total % 256 == 0 else total // 15
+    unit = 2 * TILE if total % (2 * TILE) == 0 else total // 15
     count = total // unit
     base, extra = divmod(count, parts)
     return [(base + (1 if i < extra else 0)) * unit for i in range(parts)]
@@ -36,7 +36,7 @@
     half_d, h = pieces[0].shape
 
     def kernel(*refs):
-        src, dst, (held, sem_in, sem_out) = refs[:4], refs[-4], refs[-3:]
+        src, (dst, token, held, sem_in, sem_out) = refs[:4], refs[-5:]
         dp = lax.axis_index("dp")
         x, core = dp // 2, dp % 2
         loads, stores = [], []
@@ -52,13 +52,17 @@
             store.start()
         for store in stores:
             store.wait()
+        token[...] = jnp.zeros_like(token)
 
     args = list(pieces) + ([] if out is None else [out])
     return pl.pallas_call(
         kernel,
-        out_shape=jax.ShapeDtypeStruct(shape, jnp.float32),
+        out_shape=[
+            jax.ShapeDtypeStruct(shape, jnp.float32),
+            jax.ShapeDtypeStruct((8, 128), jnp.float32),
+        ],
         in_specs=[pl.BlockSpec(memory_space=pl.ANY)] * len(args),
-        out_specs=pl.BlockSpec(memory_space=pl.ANY),
+        out_specs=[pl.BlockSpec(memory_space=pl.ANY), pl.BlockSpec(memory_space=pltpu.VMEM)],
         scratch_shapes=[
             pltpu.VMEM((4, half_d, h), jnp.float32),
             pltpu.SemaphoreType.DMA((4,)),
@@ -66,7 +70,164 @@
         ],
         compiler_params=pltpu.CompilerParams(vmem_limit_bytes=24 * 2**20),
         input_output_aliases={} if out is None else {4: 0},
-        cost_estimate=pl.CostEstimate(flops=0, bytes_accessed=32 * half_d * h, transcendentals=0),
+        cost_estimate=LIGHT,
+    )(*args)
+
+
+TILE = 256
+LIGHT = pl.CostEstimate(flops=1000, bytes_accessed=1000, transcendentals=0)
+
+
+def cost_of(products):
+    return pl.CostEstimate(flops=4 * products, bytes_accessed=1000, transcendentals=0)
+
+
+def two(v):
+    hi = v.astype(jnp.bfloat16)
+    return hi, (v - hi.astype(jnp.float32)).astype(jnp.bfloat16)
+
+
+def left3(v):
+    hi = lax.reduce_precision(v, 8, 7)
+    lo = (v - hi).astype(jnp.bfloat16)
+    hi = hi.astype(jnp.bfloat16)
+    return jnp.concatenate([hi, hi, lo], 1)
+
+
+def forward_kernel(lhs3, weight, off, wk):
+    rows, depth3 = lhs3.shape
+    depth = depth3 // 3
+    first = off // TILE
+
+    def kernel(lhs_ref, w_ref, out_ref, w3):
+        hi, lo = two(w_ref[...])
+        w3[pl.ds(0, depth), :] = hi
+        w3[pl.ds(depth, depth), :] = lo
+        w3[pl.ds(2 * depth, depth), :] = hi
+
+        out_ref[...] = jnp.dot(lhs_ref[...], w3[...], preferred_element_type=jnp.float32)
+
+    return pl.pallas_call(
+        kernel,
+        grid=(wk // TILE,),
+        in_specs=[
+            pl.BlockSpec((rows, depth3), lambda j: (0, 0), pipeline_mode=pl.Buffered(1)),
+            pl.BlockSpec((depth, TILE), lambda j: (0, first + j)),
+        ],
+        out_specs=pl.BlockSpec((rows, TILE), lambda j: (0, j)),
+        out_shape=jax.ShapeDtypeStruct((rows, wk), jnp.float32),
+        scratch_shapes=[pltpu.VMEM((depth3, TILE), jnp.bfloat16)],
+        compiler_params=pltpu.CompilerParams(vmem_limit_bytes=40 * 2**20),
+        cost_estimate=cost_of(rows * depth3 * wk),
+    )(lhs3, weight)
+
+
+def pick(own, oth, where, n, store):
+    z = where[1]
+    even = lax.rem(z, 2) == 0
+    for side, group in enumerate((own, oth)):
+        for q in range(n):
+            if q == 0:
+                v = group[0][...]
+            else:
+                below = jnp.where(even, group[n - 1 + q][...], group[q][...])
+                above = jnp.where(even, group[n - q][...], group[2 * n - 1 - q][...])
+                v = jnp.where(z >= q, below, above)
+            store(side * n + q, *two(v))
+
+
+def weight_kernel(place_of, at3, blocks, n):
+    tb, wk = blocks[0].shape
+    h = wk // 2
+    tiles = h // TILE
+    depth, toks3 = at3.shape
+    toks = toks3 // 3
+    half_d = depth // 2
+    nb = len(blocks)
+
+    def kernel(where, at_ref, *refs):
+        keep_ref, give_ref, deep = refs[-3:]
+
+        def store(q, hi, lo):
+            for i, v in enumerate((hi, lo, hi)):
+                deep[pl.ds(i * toks + q * tb, tb), :] = v
+
+        pick(refs[:nb], refs[nb : 2 * nb], where, n, store)
+        full = jnp.dot(at_ref[...], deep[...], preferred_element_type=jnp.float32)
+        keep_ref[...] = full[:half_d]
+        give_ref[...] = full[half_d:]
+
+    return pl.pallas_call(
+        kernel,
+        grid_spec=pltpu.PrefetchScalarGridSpec(
+            num_scalar_prefetch=1,
+            grid=(tiles,),
+            in_specs=[pl.BlockSpec((depth, toks3), lambda j, s: (0, 0), pipeline_mode=pl.Buffered(1))]
+            + [pl.BlockSpec((tb, TILE), lambda j, s: (0, j))] * nb
+            + [pl.BlockSpec((tb, TILE), lambda j, s: (0, tiles + j))] * nb,
+            out_specs=[pl.BlockSpec((half_d, TILE), lambda j, s: (0, j))] * 2,
+            scratch_shapes=[pltpu.VMEM((toks3, TILE), jnp.bfloat16)],
+        ),
+        out_shape=[jax.ShapeDtypeStruct((half_d, h), jnp.float32)] * 2,
+        compiler_params=pltpu.CompilerParams(vmem_limit_bytes=40 * 2**20),
+        cost_estimate=cost_of(depth * toks3 * h),
+    )(place_of, at3, *blocks, *blocks)
+
+
+def input_kernel(place_of, blocks, weight, acc, off, n):
+    tb, wk = blocks[0].shape
+    h = wk // 2
+    tiles = h // TILE
+    first = off // TILE
+    depth = weight.shape[0]
+    toks = 2 * n * tb
+    nb = len(blocks)
+    fresh = acc is None
+
+    def kernel(where, w_ref, *refs):
+        sum_ref, g_side, w_side = refs[-3:]
+
+        def store(q, hi, lo):
+            for i, v in enumerate((hi, hi, lo)):
+                g_side[pl.ds(q * tb, tb), pl.ds(i * TILE, TILE)] = v
+
+        pick(refs[:nb], refs[nb : 2 * nb], where, n, store)
+        hi, lo = two(w_ref[...])
+        for i, v in enumerate((hi, lo, hi)):
+            w_side[:, pl.ds(i * TILE, TILE)] = v
+        term = lax.dot_general(
+            g_side[...], w_side[...], (((1,), (1,)), ((), ())), preferred_element_type=jnp.float32
+        )
+
+        @pl.when(pl.program_id(0) == 0)
+        def _():
+            sum_ref[...] = term if fresh else refs[2 * nb][...] + term
+
+        @pl.when(pl.program_id(0) > 0)
+        def _():
+            sum_ref[...] = sum_ref[...] + term
+
+    whole = pl.BlockSpec((toks, depth), lambda j, s: (0, 0), pipeline_mode=pl.Buffered(1))
+    args = [place_of, weight, *blocks, *blocks] + ([] if fresh else [acc])
+    return pl.pallas_call(
+        kernel,
+        grid_spec=pltpu.PrefetchScalarGridSpec(
+            num_scalar_prefetch=1,
+            grid=(tiles,),
+            in_specs=[pl.BlockSpec((depth, TILE), lambda j, s: (0, first + s[0] * tiles + j))]
+            + [pl.BlockSpec((tb, TILE), lambda j, s: (0, j))] * nb
+            + [pl.BlockSpec((tb, TILE), lambda j, s: (0, tiles + j))] * nb
+            + ([] if fresh else [whole]),
+            out_specs=whole,
+            scratch_shapes=[
+                pltpu.VMEM((toks, 3 * TILE), jnp.bfloat16),
+                pltpu.VMEM((depth, 3 * TILE), jnp.bfloat16),
+            ],
+        ),
+        out_shape=jax.ShapeDtypeStruct((toks, depth), jnp.float32),
+        input_output_aliases={} if fresh else {len(args) - 1: 0},
+        compiler_params=pltpu.CompilerParams(vmem_limit_bytes=40 * 2**20),
+        cost_estimate=cost_of(3 * toks * depth * h),
     )(*args)
 
 
@@ -99,13 +260,29 @@
 
         widths = widths_of(ff, CHUNKS)
         offs = [sum(widths[:i]) for i in range(len(widths))]
-        up_all = [(i, i + 1) for i in range(n - 1)]
-
-        def up(v, lo, hi):
-            return lax.ppermute(v, "row", up_all[lo:hi])
-
-        def down(v, lo, hi):
-            return lax.ppermute(v, "row", [(n - 1 - i, n - 1 - j) for i, j in up_all[lo:hi]])
+        even = z % 2 == 0
+
+        def exchange(su, sd, lo, hi):
+            pairs = ([], [])
+            for i in range(lo, hi):
+                pairs[i % 2].append((i, i + 1))
+                pairs[(n - 2 - i) % 2].append((n - 1 - i, n - 2 - i))
+            first, second = (su, su) if su is sd else (jnp.where(even, su, sd), jnp.where(even, sd, su))
+            return [
+                lax.ppermute(v, "row", p) if p else jnp.zeros_like(v)
+                for v, p in zip((first, second), pairs)
+            ]
+
+        def came(pair):
+            return [jnp.where(even, pair[1], pair[0]), jnp.where(even, pair[0], pair[1])]
+
+        halves = jnp.stack([both[:, :half_d], both[:, half_d:]])
+        both = jnp.concatenate([halves[core], halves[1 - core]], 1)
+        kernels = ff % (2 * TILE) == 0 and depth % (2 * TILE) == 0 and tokens % TILE == 0
+        own_in = own
+        if kernels:
+            own_in, at3 = left3(own), left3(both.T)
+            place_of = jnp.stack([x, z]).astype(jnp.int32)
 
         count = len(widths)
         part, acts, wg, got, ig_terms = {}, {}, {}, {}, []
@@ -114,10 +291,13 @@
         def forward(k):
             def run(lhs):
                 off, wk = offs[k], widths[k]
-                part[k] = mm(lhs, weight[:, off : off + wk], ((1,), (0,))).reshape(n, tb, wk)
+                if kernels:
+                    part[k] = forward_kernel(lhs, weight, off, wk).reshape(n, tb, wk)
+                else:
+                    part[k] = mm(lhs, weight[:, off : off + wk], ((1,), (0,))).reshape(n, tb, wk)
                 return [part[k]]
 
-            return (lambda: [own]), run
+            return (lambda: [own_in]), run
 
         def weight_product(k):
             def ins():
@@ -126,12 +306,16 @@
 
             def run(g, *recv):
                 h = widths[k] // 2
-                ups, dns = recv[: n - 1], recv[n - 1 :]
+                if kernels:
+                    keep, give = weight_kernel(place_of, at3, [g, *recv], n)
+                    wg[k] = {"keep": keep, "in": lax.ppermute(give, "dp", swap_core)}
+                    return [keep]
+                pairs = [came(v) for v in zip(recv[: n - 1], recv[n - 1 :])]
+                ups, dns = [v[0] for v in pairs], [v[1] for v in pairs]
                 blocks = [g] + [jnp.where(z > t, ups[t], dns[n - 2 - t]) for t in range(n - 1)]
                 gz = jnp.concatenate([v[:, :h] for v in blocks] + [v[:, h:] for v in blocks], 0)
                 full = mm(both, gz, ((0,), (0,)))
-                keep = lax.dynamic_slice_in_dim(full, core * half_d, half_d, 0)
-                give = lax.dynamic_slice_in_dim(full, (1 - core) * half_d, half_d, 0)
+                keep, give = full[:half_d], full[half_d:]
                 wg[k] = {"gz": gz, "keep": keep, "in": lax.ppermute(give, "dp", swap_core)}
                 return [keep]
 
@@ -166,8 +350,8 @@
         def weight_place(k):
             def run(*pieces):
                 if ff % 256 == 0:
-                    out["wg"] = place(out.get("wg"), pieces, offs[k], (depth, ff))
-                    return []
+                    out["wg"], token = place(out.get("wg"), pieces, offs[k], (depth, ff))
+                    return [token]
                 if "wg" not in out:
                     out["wg"] = jnp.zeros((depth, ff), jnp.float32)
                 for i, piece in enumerate(pieces):
@@ -188,35 +372,43 @@
 
             return (lambda: [wg[k]["gz"]]), run
 
+        def input_blocks(k):
+            def run(*blocks):
+                out["ig"] = input_kernel(place_of, blocks, weight, out.get("ig"), offs[k], n)
+                return [out["ig"]]
+
+            return weight_product(k)[0], run
+
         events = {}
         for k in range(count):
             s, j = k % 2, k // 2
             first = 2 * j * n + s
             end = first + 4 * n - 4
-            plan = [(first - 1, forward(k)), (end, weight_product(k)), (end + 1, weight_sum(k))]
             last = k >= count - 2
+            plan = [(end if last else end + 5, input_blocks(k))] if kernels else []
+            plan += [(first - (1 if k < 2 else 2), forward(k)), (end, weight_product(k))]
+            plan += [(end + (1 if last else 2), weight_sum(k))]
             cross = end + 1 if last else end + 4 + s
             plan += [] if last else [(cross, weight_cross(k))]
-            plan += [(end + (2 if last else 5), input_product(k))]
-            plan += [(cross + (1 if last else 3), weight_back(k)), (cross + (2 if last else 4), weight_place(k))]
+            plan += [] if kernels else [(end + (2 if last else 5), input_product(k))]
+            plan += [(cross + (1 if last else 2), weight_back(k)), (cross + (2 if last else 3), weight_place(k))]
             for when, what in plan:
                 events.setdefault(when, []).append(what)
 
-        done = []
+        done, before = [], []
 
         def half_slot(h, recv):
-            nonlocal done
             todo = events.pop(h, [])
             ins = [what[0]() for what in todo]
             flat = tuple(v for group in ins for v in group)
-            tied = lax.optimization_barrier(tuple(recv) + tuple(done) + flat)
+            tied = lax.optimization_barrier(tuple(recv) + tuple(before) + flat)
             new = list(tied[: len(recv)])
-            flat = list(tied[len(recv) + len(done) :])
+            flat = list(tied[len(recv) + len(before) :])
             return new, todo, ins, flat
 
         def work(todo, ins, flat):
-            nonlocal done
-            done = []
+            nonlocal done, before
+            done, before = [], done
             for what, group in zip(todo, ins):
                 take, flat = flat[: len(group)], flat[len(group) :]
                 done += what[1](*take)
@@ -243,6 +435,7 @@
             new, todo, ins, flat = half_slot(h, recv)
             ag = new[:2] if st["ag"] else []
             rs = (ag if same else new[len(ag) :]) if st["rs"] else []
+            ag, rs = (came(v) if v else [] for v in (ag, rs))
             st["rs"], st["ag"] = [], []
             if t < n - 1:
                 has_rs = cur is not None
@@ -255,13 +448,13 @@
                     base = ag if t == 0 else rs
                     su = base[0] + jnp.where(z <= t, blk_u, 0.0)
                     sd = base[1] + jnp.where(n - 1 - z <= t, blk_d, 0.0)
-                    st["rs"] = st["ag"] = [up(su, 0, n - 1), down(sd, 0, n - 1)]
+                    st["rs"] = st["ag"] = exchange(su, sd, 0, n - 1)
                 else:
                     if has_rs:
                         su, sd = (blk_u, blk_d) if t == 0 else (rs[0] + blk_u, rs[1] + blk_d)
-                        st["rs"] = [up(su, 0, t + 1), down(sd, 0, t + 1)]
+                        st["rs"] = exchange(su, sd, 0, t + 1)
                     if has_ag:
-                        st["ag"] = [up(ag[0], t + 1, n - 1), down(ag[1], t + 1, n - 1)]
+                        st["ag"] = exchange(ag[0], ag[1], t + 1, n - 1)
             elif cur is not None:
                 pre = lax.dynamic_index_in_dim(part[cur], z, 0, keepdims=False) + rs[0] + rs[1]
                 off, wk = offs[cur], widths[cur]
@@ -274,7 +467,7 @@
                 theirs = jnp.where(x == 0, right, left)
                 g = jnp.concatenate([mine, lax.ppermute(theirs, "dp", swap_x)], 1)
                 got[cur] = {"g": g, "ups": [], "dns": []}
-                st["ag"] = [up(g, 0, n - 1), down(g, 0, n - 1)]
+                st["ag"] = exchange(g, g, 0, n - 1)
             work(todo, ins, flat)
         for s in (0, 1):
             if state[s]["ag"]:
@@ -287,13 +480,18 @@
         acts = [acts[k] for k in range(count)]
 
         ig = ig.reshape(2, n, tb, depth)
-        mine = ig[0] + lax.ppermute(ig[1], "dp", swap_x)
-        if ncol != 2:
-            mine = lax.psum_scatter(mine, "col", scatter_dimension=2, tiled=True)
-        else:
-            keep = lax.dynamic_slice_in_dim(mine, y * half_d, half_d, 2)
-            give = lax.dynamic_slice_in_dim(mine, (1 - y) * half_d, half_d, 2)
-            mine = keep + lax.ppermute(give, "col", swap_y)
+        def over_x(v):
+            return v[0] + lax.ppermute(v[1], "dp", swap_x)
+
+        def over_y(v):
+            if ncol != 2:
+                return lax.psum_scatter(v, "col", scatter_dimension=v.ndim - 1, tiled=True)
+            left, right = v[..., :half_d], v[..., half_d:]
+            keep, give = jnp.where(y == 0, left, right), jnp.where(y == 0, right, left)
+            return keep + lax.ppermute(give, "col", swap_y)
+
+        mid = n // 2
+        mine = jnp.concatenate([over_y(over_x(ig[:, :mid])), over_x(over_y(ig[:, mid:]))], 0)
         input_grad = unrotate(mine, z, n).reshape(tokens, -1)
         return jnp.concatenate(acts, 1), input_grad, wg_out
 

time: 738 us -> 693 us (0.939)
  Pallas kernels: 21.8 us -> 158 us
  matrix products: 126 us -> 0 us
  waiting for transfers between devices: 302 us -> 235 us
  starting transfers between devices: 190 us -> 201 us
  other arithmetic: 59 us -> 67.4 us
    pallas_call x6 -> x32, Pallas kernels: 21.8 us -> 158 us  [the longest x8 49.7 us: input_kernel(): pl.pallas_call(kernel, grid_spec=pltpu.PrefetchScalarGridSpec(num_scalar_...]
    dot_general x18 -> x0, matrix products: 126 us -> none  [mm(): lax.dot_general(lhs, rhs, (contract, ((), ())), precision=HIGH, preferred...]
    ppermute x64 -> x82, waiting for transfers between devices: 219 us -> 147 us  [the longest x70 147 us: exchange(): lax.ppermute(v, 'row', p)]
    add x18 -> x4, other arithmetic: 17.4 us -> 0.75 us  [the longest x2 0.49 us: over_y(): return keep + lax.ppermute(give, 'col', swap_y)]
    select_n x17 -> x42, other arithmetic: 5.71 us -> 18.3 us  [the longest x24 14.6 us: exchange(): jnp.where(even, sd, su)]
    mul x3 -> x5, other arithmetic: 9.62 us -> 15.6 us  [body(): grad = cot[:, off:off + wk] * (sig * (1.0 + pre * (1.0 - sig)))]
    ppermute x6 -> x8, waiting for transfers between devices: 39.3 us -> 42.9 us  [run(): wg[k]['x'] = lax.ppermute(keep, 'dp', swap_x)]
    ppermute x6 -> x8, waiting for transfers between devices: 20 us -> 23.3 us  [body(): g = jnp.concatenate([mine, lax.ppermute(theirs, 'dp', swap_x)], 1)]
  transfers between devices with their start and end apart: 91 -> 117, of which waited for: 44 -> 39; matrix products, arithmetic and copies ran while one was open for 22% -> 9% of each run, Pallas kernels for 3% -> 23%
where the time goes in v2:
time: 693 us; the launch traced here: 686 us
  waiting for transfers between devices  235 us (34%)
  starting transfers between devices  201 us (29%)
  Pallas kernels  158 us (23%)
  other arithmetic  67.4 us (10%)
  local copies, waits for them, and re-layouts  20.8 us (3%)
    ppermute x70, starting transfers between devices, exchange(): lax.ppermute(v, 'row', p)  160 us
    ppermute x70, waiting for transfers between devices, exchange(): lax.ppermute(v, 'row', p)  147 us
    pallas_call x8, Pallas kernels, input_kernel(): pl.pallas_call(kernel, grid_spec=pltpu.PrefetchScalarGridSpec(num_scalar_...  49.7 us
    ppermute x8, waiting for transfers between devices, run(): wg[k]['x'] = lax.ppermute(keep, 'dp', swap_x)  42.9 us
    pallas_call x8, Pallas kernels, forward_kernel(): pl.pallas_call(kernel, grid=(wk // TILE,), in_specs=[pl.BlockSpec((rows,...  42.3 us
    pallas_call x8, Pallas kernels, weight_kernel(): pl.pallas_call(kernel, grid_spec=pltpu.PrefetchScalarGridSpec(num_scalar_...  38.4 us
    pallas_call x8, Pallas kernels, place(): pl.pallas_call(kernel, out_shape=[jax.ShapeDtypeStruct(shape, jnp.float32...  27.9 us
    ppermute x8, waiting for transfers between devices, body(): g = jnp.concatenate([mine, lax.ppermute(theirs, 'dp', swap_x)], 1)  23.3 us
  transfers between devices with their start and end apart: 117, of which 39 were waited for; matrix products, arithmetic and copies ran while one was open for 9% of the time, Pallas kernels for 23%

profile of v2, /device:TPU:0, one launch (start us, length us, event | category | flops | bytes accessed | tf_op | source)
XLA Modules:
  0.0 686.3 jit_solution(481123075276369253)
XLA Ops:
  5.2 21.9 %collective-permute-done = f32[512,512]{1,0:T(8,128)S(1)} collective-permute-done((f32[512,512]{1,0:T(8,128)}, f32[512,512]{1,0:T(8,128)S(1)}, u32[]{:S(2)}, u32[]{:S(2)}) %collective-permute-start) | collective-permute-done | bytes 1048608 | tf_op jit(solution)/shard_map/ppermute | solution.py:253
  114.4 6.0 multiply_multiply_fusion.5
  157.8 5.9 collective-permute-done.14.refs_2_.refs_9_
  209.7 10.3 %collective-permute-done.30 = f32[128,1024]{1,0:T(8,128)S(1)} collective-permute-done((f32[128,1024]{1,0:T(8,128)S(1)}, f32[128,1024]{1,0:T(8,128)S(1)}, u32[]{:S(2)}, u32[]{:S(2)}) %collective-permute-start.30) | collective-permute-done | bytes 524320 | tf_op jit(solution)/shard_map/ppermute | solution.py:272
  232.4 8.9 %collective-permute-start.34 = (f32[128,1024]{1,0:T(8,128)S(1)}, f32[128,1024]{1,0:T(8,128)S(1)}, u32[]{:S(2)}, u32[]{:S(2)}) collective-permute-start(f32[128,1024]{1,0:T(8,128)S(1)} %pad_maximum_fusion.7.refs_0_.refs_7_), channel_id=1, source_target_pairs={{0,2},{6,4},{4,6},{2,0},{1,3},{7,5},{5,7},{3,1},{8,10},{14,12},{12... | collective-permute-start | bytes 1572872 | tf_op jit(solution)/shard_map/ppermute | solution.py:272
  278.8 6.3 shard_map.66.refs_14_
  292.6 6.6 shard_map.67.refs_14_
  304.0 7.1 %collective-permute-done.44.refs_2_ = f32[512,512]{1,0:T(8,128)} collective-permute-done((f32[512,512]{1,0:T(8,128)}, f32[512,512]{1,0:T(8,128)}, u32[]{:S(2)}, u32[]{:S(2)}) %collective-permute-start.44) | collective-permute-done | bytes 1048608 | tf_op jit(solution)/shard_map/ppermute | solution.py:337
  343.5 11.6 %collective-permute-done.56 = f32[128,1024]{1,0:T(8,128)S(1)} collective-permute-done((f32[128,1024]{1,0:T(8,128)S(1)}, f32[128,1024]{1,0:T(8,128)S(1)}, u32[]{:S(2)}, u32[]{:S(2)}) %collective-permute-start.56) | collective-permute-done | bytes 524320 | tf_op jit(solution)/shard_map/ppermute | solution.py:272
  360.1 7.1 %collective-permute-done.59 = f32[128,512]{1,0:T(8,128)S(1)} collective-permute-done((f32[128,512]{1,0:T(8,128)S(1)}, f32[128,512]{1,0:T(8,128)S(1)}, u32[]{:S(2)}, u32[]{:S(2)}) %collective-permute-start.59) | collective-permute-done | bytes 262176 | tf_op jit(solution)/shard_map/ppermute | solution.py:468
  367.2 11.2 %collective-permute-start.60 = (f32[128,1024]{1,0:T(8,128)S(1)}, f32[128,1024]{1,0:T(8,128)S(1)}, u32[]{:S(2)}, u32[]{:S(2)}) collective-permute-start(f32[128,1024]{1,0:T(8,128)S(1)} %pad_maximum_fusion.9.refs_0_.refs_7_), channel_id=1, source_target_pairs={{0,2},{6,4},{4,6},{2,0},{1,3},{7,5},{5,7},{3,1},{8,10},{14,12},{12... | collective-permute-start | bytes 1572872 | tf_op jit(solution)/shard_map/ppermute | solution.py:272
  414.5 6.6 shard_map.72.refs_14_
  435.3 6.7 shard_map.73.refs_14_
  463.5 11.9 %collective-permute-done.79.refs_3_.refs_10_ = f32[128,1024]{1,0:T(8,128)S(1)} collective-permute-done((f32[128,1024]{1,0:T(8,128)S(1)}, f32[128,1024]{1,0:T(8,128)S(1)}, u32[]{:S(2)}, u32[]{:S(2)}) %collective-permute-start.79) | collective-permute-done | bytes 524320 | tf_op jit(solution)/shard_map/ppermute | solution.py:272
  475.5 11.0 %collective-permute-done.71 = f32[128,1024]{1,0:T(8,128)S(1)} collective-permute-done((f32[128,1024]{1,0:T(8,128)S(1)}, f32[128,1024]{1,0:T(8,128)S(1)}, u32[]{:S(2)}, u32[]{:S(2)}) %collective-permute-start.71) | collective-permute-done | bytes 524320 | tf_op jit(solution)/shard_map/ppermute | solution.py:272
  504.8 8.1 %collective-permute-done.89.refs_1_.refs_8_ = f32[128,1024]{1,0:T(8,128)S(1)} collective-permute-done((f32[128,1024]{1,0:T(8,128)S(1)}, f32[128,1024]{1,0:T(8,128)S(1)}, u32[]{:S(2)}, u32[]{:S(2)}) %collective-permute-start.89) | collective-permute-done | bytes 524320 | tf_op jit(solution)/shard_map/ppermute | solution.py:272
  522.6 14.3 %collective-permute-done.94 = f32[128,256]{1,0:T(8,128)S(1)} collective-permute-done((f32[128,256]{1,0:T(8,128)S(1)}, f32[128,256]{1,0:T(8,128)S(1)}, u32[]{:S(2)}, u32[]{:S(2)}) %collective-permute-start.94) | collective-permute-done | bytes 131104 | tf_op jit(solution)/shard_map/ppermute | solution.py:468
  550.0 6.5 shard_map.76.refs_14_
  559.6 6.6 shard_map.77.refs_14_
  566.2 10.4 %collective-permute-done.98.refs_3_.refs_10_ = f32[128,1024]{1,0:T(8,128)S(1)} collective-permute-done((f32[128,1024]{1,0:T(8,128)S(1)}, f32[128,1024]{1,0:T(8,128)S(1)}, u32[]{:S(2)}, u32[]{:S(2)}) %collective-permute-start.98) | collective-permute-done | bytes 524320 | tf_op jit(solution)/shard_map/ppermute | solution.py:272
  584.7 7.9 %collective-permute-done.105.refs_3_.refs_10_ = f32[128,512]{1,0:T(8,128)S(1)} collective-permute-done((f32[128,512]{1,0:T(8,128)S(1)}, f32[128,512]{1,0:T(8,128)S(1)}, u32[]{:S(2)}, u32[]{:S(2)}) %collective-permute-start.105) | collective-permute-done | bytes 262176 | tf_op jit(solution)/shard_map/ppermute | solution.py:272
  598.0 6.6 shard_map.79.refs_14_
  605.2 12.3 %collective-permute-done.110.refs_2_ = f32[512,512]{1,0:T(8,128)S(1)} collective-permute-done((f32[512,512]{1,0:T(8,128)S(1)}, f32[512,512]{1,0:T(8,128)S(1)}, u32[]{:S(2)}, u32[]{:S(2)}) %collective-permute-start.110) | collective-permute-done | bytes 1048608 | tf_op jit(solution)/shard_map/ppermute | solution.py:329
  640.3 18.1 %collective-permute-done.115.refs_2_ = f32[512,256]{1,0:T(8,128)S(1)} collective-permute-done((f32[512,256]{1,0:T(8,128)S(1)}, f32[512,256]{1,0:T(8,128)S(1)}, u32[]{:S(2)}, u32[]{:S(2)}) %collective-permute-start.115) | collective-permute-done | bytes 524320 | tf_op jit(solution)/shard_map/ppermute | solution.py:329
  (609 shorter events, 452.8 us)
Async XLA Ops:
  0.6 26.4 %collective-permute-start = (f32[512,512]{1,0:T(8,128)}, f32[512,512]{1,0:T(8,128)S(1)}, u32[]{:S(2)}, u32[]{:S(2)}) collective-permute-start(f32[512,512]{1,0:T(8,128)} %param.3), channel_id=1, source_target_pairs={{0,1},{1,0},{2,3},{3,2},{4,5},{5,4},{6,7},{7,6},{8,9},{9,8},{10,11... | collective-permute-start | bytes 3145736 | tf_op jit(solution)/shard_map/ppermute | solution.py:253
  3.7 43.0 %collective-permute-start.20 = (f32[512,512]{1,0:T(8,128)}, f32[512,512]{1,0:T(8,128)}, u32[]{:S(2)}, u32[]{:S(2)}) collective-permute-start(f32[512,512]{1,0:T(8,128)} %param.3), channel_id=1, source_target_pairs={{0,16},{16,0},{8,24},{24,8},{1,17},{17,1},{9,25},{25,9},{2,18},{18... | collective-permute-start | bytes 3145736 | tf_op jit(solution)/shard_map/ppermute | solution.py:257
  46.6 32.5 %collective-permute-start.21 = (f32[512,512]{1,0:T(8,128)}, f32[512,512]{1,0:T(8,128)S(1)}, u32[]{:S(2)}, u32[]{:S(2)}) collective-permute-start(f32[512,512]{1,0:T(8,128)} %collective-permute-done.20), channel_id=1, source_target_pairs={{0,1},{1,0},{2,3},{3,2},{4,5},{5,4},{6,7},{7,6},{8,9},{9,8},{10,11... | collective-permute-start | bytes 3145736 | tf_op jit(solution)/shard_map/ppermute | solution.py:253
  75.2 39.2 %collective-permute-start.4 = (f32[128,1024]{1,0:T(8,128)}, f32[128,1024]{1,0:T(8,128)}, u32[]{:S(2)}, u32[]{:S(2)}) collective-permute-start(f32[128,1024]{1,0:T(8,128)} %get-tuple-element.624), channel_id=1, source_target_pairs={{0,2},{6,4},{4,6},{2,0},{1,3},{7,5},{5,7},{3,1},{8,10},{14,12},{12... | collective-permute-start | bytes 1572872 | tf_op jit(solution)/shard_map/ppermute | solution.py:272
  77.7 36.7 %collective-permute-start.5 = (f32[128,1024]{1,0:T(8,128)}, f32[128,1024]{1,0:T(8,128)}, u32[]{:S(2)}, u32[]{:S(2)}) collective-permute-start(f32[128,1024]{1,0:T(8,128)} %get-tuple-element.623), channel_id=1, source_target_pairs={{2,4},{4,2},{3,5},{5,3},{10,12},{12,10},{11,13},{13,11},{18,20},{2... | collective-permute-start | bytes 1572872 | tf_op jit(solution)/shard_map/ppermute | solution.py:272
  86.5 27.9 %collective-permute-start.10 = (f32[128,1024]{1,0:T(8,128)}, f32[128,1024]{1,0:T(8,128)}, u32[]{:S(2)}, u32[]{:S(2)}) collective-permute-start(f32[128,1024]{1,0:T(8,128)} %get-tuple-element.619), channel_id=1, source_target_pairs={{2,4},{4,2},{3,5},{5,3},{10,12},{12,10},{11,13},{13,11},{18,20},{2... | collective-permute-start | bytes 1572872 | tf_op jit(solution)/shard_map/ppermute | solution.py:272
  231.8 56.3 %collective-permute-start.50 = (f32[512,512]{1,0:T(8,128)S(1)}, f32[512,512]{1,0:T(8,128)S(1)}, u32[]{:S(2)}, u32[]{:S(2)}) collective-permute-start(f32[512,512]{1,0:T(8,128)S(1)} %add.471.refs_0_), channel_id=1, source_target_pairs={{0,8},{8,0},{16,24},{24,16},{1,9},{9,1},{17,25},{25,17},{2,10},{10... | collective-permute-start | bytes 3145736 | tf_op jit(solution)/shard_map/ppermute | solution.py:330
  288.1 39.5 %collective-permute-start.54 = (f32[512,512]{1,0:T(8,128)}, f32[512,512]{1,0:T(8,128)}, u32[]{:S(2)}, u32[]{:S(2)}) collective-permute-start(f32[512,512]{1,0:T(8,128)} %add.474.refs_0_), channel_id=1, source_target_pairs={{0,8},{8,0},{16,24},{24,16},{1,9},{9,1},{17,25},{25,17},{2,10},{10... | collective-permute-start | bytes 3145736 | tf_op jit(solution)/shard_map/ppermute | solution.py:330
  359.7 26.4 %collective-permute-start.67 = (f32[128,512]{1,0:T(8,128)S(1)}, f32[128,512]{1,0:T(8,128)S(1)}, u32[]{:S(2)}, u32[]{:S(2)}) collective-permute-start(f32[128,512]{1,0:T(8,128)S(1)} %get-tuple-element.642), channel_id=1, source_target_pairs={{0,16},{16,0},{8,24},{24,8},{1,17},{17,1},{9,25},{25,9},{2,18},{18... | collective-permute-start | bytes 786440 | tf_op jit(solution)/shard_map/ppermute | solution.py:468
  423.3 32.8 %collective-permute-start.82 = (f32[512,512]{1,0:T(8,128)}, f32[512,512]{1,0:T(8,128)}, u32[]{:S(2)}, u32[]{:S(2)}) collective-permute-start(f32[512,512]{1,0:T(8,128)} %add.496.refs_0_), channel_id=1, source_target_pairs={{0,8},{8,0},{16,24},{24,16},{1,9},{9,1},{17,25},{25,17},{2,10},{10... | collective-permute-start | bytes 3145736 | tf_op jit(solution)/shard_map/ppermute | solution.py:330
  430.5 27.1 %collective-permute-start.80 = (f32[128,512]{1,0:T(8,128)}, f32[128,512]{1,0:T(8,128)}, u32[]{:S(2)}, u32[]{:S(2)}) collective-permute-start(f32[128,512]{1,0:T(8,128)} %get-tuple-element.632), channel_id=1, source_target_pairs={{0,2},{6,4},{1,3},{7,5},{8,10},{14,12},{9,11},{15,13},{16,18},{22,... | collective-permute-start | bytes 786440 | tf_op jit(solution)/shard_map/ppermute | solution.py:272
  447.3 28.1 %collective-permute-start.83 = (f32[512,512]{1,0:T(8,128)}, f32[512,512]{1,0:T(8,128)S(1)}, u32[]{:S(2)}, u32[]{:S(2)}) collective-permute-start(f32[512,512]{1,0:T(8,128)} %collective-permute-done.70.refs_2_), channel_id=1, source_target_pairs={{0,8},{8,0},{16,24},{24,16},{1,9},{9,1},{17,25},{25,17},{2,10},{10... | collective-permute-start | bytes 3145736 | tf_op jit(solution)/shard_map/ppermute | solution.py:345
  455.0 31.5 %collective-permute-start.73 = (f32[512,512]{1,0:T(8,128)S(1)}, f32[512,512]{1,0:T(8,128)S(1)}, u32[]{:S(2)}, u32[]{:S(2)}) collective-permute-start(f32[512,512]{1,0:T(8,128)S(1)} %get-tuple-element.419), channel_id=1, source_target_pairs={{0,8},{8,0},{16,24},{24,16},{1,9},{9,1},{17,25},{25,17},{2,10},{10... | collective-permute-start | bytes 3145736 | tf_op jit(solution)/shard_map/ppermute | solution.py:311
  457.6 29.0 %collective-permute-start.71 = (f32[128,1024]{1,0:T(8,128)S(1)}, f32[128,1024]{1,0:T(8,128)S(1)}, u32[]{:S(2)}, u32[]{:S(2)}) collective-permute-start(f32[128,1024]{1,0:T(8,128)S(1)} %get-tuple-element.610), channel_id=1, source_target_pairs={{0,2},{6,4},{4,6},{2,0},{1,3},{7,5},{5,7},{3,1},{8,10},{14,12},{12... | collective-permute-start | bytes 1572872 | tf_op jit(solution)/shard_map/ppermute | solution.py:272
  512.9 31.9 %collective-permute-start.93 = (f32[512,512]{1,0:T(8,128)S(1)}, f32[512,512]{1,0:T(8,128)S(1)}, u32[]{:S(2)}, u32[]{:S(2)}) collective-permute-start(f32[512,512]{1,0:T(8,128)S(1)} %add.514.refs_0_), channel_id=1, source_target_pairs={{0,16},{16,0},{8,24},{24,8},{1,17},{17,1},{9,25},{25,9},{2,18},{18... | collective-permute-start | bytes 3145736 | tf_op jit(solution)/shard_map/ppermute | solution.py:337
  514.6 30.1 %collective-permute-start.91 = (f32[128,1024]{1,0:T(8,128)S(1)}, f32[128,1024]{1,0:T(8,128)S(1)}, u32[]{:S(2)}, u32[]{:S(2)}) collective-permute-start(f32[128,1024]{1,0:T(8,128)S(1)} %get-tuple-element.634), channel_id=1, source_target_pairs={{4,6},{2,0},{5,7},{3,1},{12,14},{10,8},{13,15},{11,9},{20,22},{18,... | collective-permute-start | bytes 1572872 | tf_op jit(solution)/shard_map/ppermute | solution.py:272
  516.9 27.8 %collective-permute-start.92 = (f32[128,1024]{1,0:T(8,128)S(1)}, f32[128,1024]{1,0:T(8,128)S(1)}, u32[]{:S(2)}, u32[]{:S(2)}) collective-permute-start(f32[128,1024]{1,0:T(8,128)S(1)} %get-tuple-element.633), channel_id=1, source_target_pairs={{2,4},{4,2},{3,5},{5,3},{10,12},{12,10},{11,13},{13,11},{18,20},{2... | collective-permute-start | bytes 1572872 | tf_op jit(solution)/shard_map/ppermute | solution.py:272
  548.3 28.3 %collective-permute-start.97 = (f32[512,512]{1,0:T(8,128)S(1)}, f32[512,512]{1,0:T(8,128)}, u32[]{:S(2)}, u32[]{:S(2)}) collective-permute-start(f32[512,512]{1,0:T(8,128)S(1)} %add.512.refs_0_), channel_id=1, source_target_pairs={{0,16},{16,0},{8,24},{24,8},{1,17},{17,1},{9,25},{25,9},{2,18},{18... | collective-permute-start | bytes 3145736 | tf_op jit(solution)/shard_map/ppermute | solution.py:337
  556.7 28.0 %collective-permute-start.87 = (f32[512,512]{1,0:T(8,128)S(1)}, f32[512,512]{1,0:T(8,128)S(1)}, u32[]{:S(2)}, u32[]{:S(2)}) collective-permute-start(f32[512,512]{1,0:T(8,128)S(1)} %add.512.refs_0_), channel_id=1, source_target_pairs={{0,8},{8,0},{16,24},{24,16},{1,9},{9,1},{17,25},{25,17},{2,10},{10... | collective-permute-start | bytes 3145736 | tf_op jit(solution)/shard_map/ppermute | solution.py:330
  604.6 35.6 %collective-permute-start.113 = (f32[512,512]{1,0:T(8,128)S(1)}, f32[512,512]{1,0:T(8,128)S(1)}, u32[]{:S(2)}, u32[]{:S(2)}) collective-permute-start(f32[512,512]{1,0:T(8,128)S(1)} %add.520.refs_0_), channel_id=1, source_target_pairs={{0,8},{8,0},{16,24},{24,16},{1,9},{9,1},{17,25},{25,17},{2,10},{10... | collective-permute-start | bytes 3145736 | tf_op jit(solution)/shard_map/ppermute | solution.py:330
  617.5 40.9 %collective-permute-start.114 = (f32[512,512]{1,0:T(8,128)S(1)}, f32[512,512]{1,0:T(8,128)S(1)}, u32[]{:S(2)}, u32[]{:S(2)}) collective-permute-start(f32[512,512]{1,0:T(8,128)S(1)} %collective-permute-done.110.refs_2_), channel_id=1, source_target_pairs={{0,8},{8,0},{16,24},{24,16},{1,9},{9,1},{17,25},{25,17},{2,10},{10... | collective-permute-start | bytes 3145736 | tf_op jit(solution)/shard_map/ppermute | solution.py:345
  621.5 36.9 %collective-permute-start.106 = (f32[2,128,1024]{2,1,0:T(8,128)S(1)}, f32[2,128,1024]{2,1,0:T(8,128)S(1)}, u32[]{:S(2)}, u32[]{:S(2)}) collective-permute-start(f32[2,128,1024]{2,1,0:T(8,128)S(1)} %slice_bitcast_fusion), channel_id=1, source_target_pairs={{0,16},{16,0},{8,24},{24,8},{1,17},{17,1},{9,25},{25,9},{2,18},{18... | collective-permute-start | bytes 3145736 | tf_op jit(solution)/shard_map/ppermute | solution.py:484
  633.7 26.6 %collective-permute-start.108 = (f32[2,2,128,512]{3,2,1,0:T(8,128)S(1)}, f32[2,2,128,512]{3,2,1,0:T(8,128)S(1)}, u32[]{:S(2)}, u32[]{:S(2)}) collective-permute-start(f32[2,2,128,512]{3,2,1,0:T(8,128)S(1)} %slice_select_fusion), channel_id=1, source_target_pairs={{0,1},{1,0},{2,3},{3,2},{4,5},{5,4},{6,7},{7,6},{8,9},{9,8},{10,11... | collective-permute-start | bytes 3145736 | tf_op jit(solution)/shard_map/ppermute | solution.py:491
  640.2 39.2 %collective-permute-start.112 = (f32[512,256]{1,0:T(8,128)S(1)}, f32[512,256]{1,0:T(8,128)S(1)}, u32[]{:S(2)}, u32[]{:S(2)}) collective-permute-start(f32[512,256]{1,0:T(8,128)S(1)} %add.521.refs_0_), channel_id=1, source_target_pairs={{0,8},{8,0},{16,24},{24,16},{1,9},{9,1},{17,25},{25,17},{2,10},{10... | collective-permute-start | bytes 1572872 | tf_op jit(solution)/shard_map/ppermute | solution.py:330
  (223 other events, 3762.0 us)

commit v3 on v2

--- a/solution.py
+++ b/solution.py
@@ -32,7 +32,7 @@
     return lax.optimization_barrier((value,) + others)
 
 
-def place(out, pieces, off, shape):
+def place(out, after, pieces, off, shape):
     half_d, h = pieces[0].shape
 
     def kernel(*refs):
@@ -54,7 +54,7 @@
             store.wait()
         token[...] = jnp.zeros_like(token)
 
-    args = list(pieces) + ([] if out is None else [out])
+    args = list(pieces) + ([] if out is None else [out, after])
     return pl.pallas_call(
         kernel,
         out_shape=[
@@ -350,8 +350,10 @@
         def weight_place(k):
             def run(*pieces):
                 if ff % 256 == 0:
-                    out["wg"], token = place(out.get("wg"), pieces, offs[k], (depth, ff))
-                    return [token]
+                    out["wg"], out["after"] = place(
+                        out.get("wg"), out.get("after"), pieces, offs[k], (depth, ff)
+                    )
+                    return [out["after"]]
                 if "wg" not in out:
                     out["wg"] = jnp.zeros((depth, ff), jnp.float32)
                 for i, piece in enumerate(pieces):
@@ -391,7 +393,8 @@
             cross = end + 1 if last else end + 4 + s
             plan += [] if last else [(cross, weight_cross(k))]
             plan += [] if kernels else [(end + (2 if last else 5), input_product(k))]
-            plan += [(cross + (1 if last else 2), weight_back(k)), (cross + (2 if last else 3), weight_place(k))]
+            when = cross + 2 if last else max(cross + 3, 2 * n * ((count + 1) // 2) - 2 + k)
+            plan += [(cross + (1 if last else 2), weight_back(k)), (when, weight_place(k))]
             for when, what in plan:
                 events.setdefault(when, []).append(what)
 
@@ -403,6 +406,9 @@
             flat = tuple(v for group in ins for v in group)
             tied = lax.optimization_barrier(tuple(recv) + tuple(before) + flat)
             new = list(tied[: len(recv)])
+            for was, now in zip(before, tied[len(recv) :]):
+                if was is out.get("after"):
+                    out["after"] = now
             flat = list(tied[len(recv) + len(before) :])
             return new, todo, ins, flat
 

time: 693 us -> 676 us (0.975)
  waiting for transfers between devices: 235 us -> 214 us
  local copies, waits for them, and re-layouts: 20.8 us -> 33.2 us
    ppermute x2, waiting for transfers between devices: 0.01 us -> 23.8 us  [over_x(): return v[0] + lax.ppermute(v[1], 'dp', swap_x)]
    ppermute x8, waiting for transfers between devices: 23.3 us -> 4.54 us  [body(): g = jnp.concatenate([mine, lax.ppermute(theirs, 'dp', swap_x)], 1)]
    ppermute x70, waiting for transfers between devices: 147 us -> 130 us  [exchange(): lax.ppermute(v, 'row', p)]
    unnamed x262 -> x242, local copies, waits for them, and re-layouts: 12.9 us -> 25.5 us
    ppermute x8, waiting for transfers between devices: 42.9 us -> 33.4 us  [run(): wg[k]['x'] = lax.ppermute(keep, 'dp', swap_x)]
  transfers between devices with their start and end apart: 117 -> 117, of which waited for: 39 -> 36; matrix products, arithmetic and copies ran while one was open for 9% -> 10% of each run, Pallas kernels for 23% -> 22%
where the time goes in v3:
time: 676 us; the launch traced here: 669 us
  waiting for transfers between devices  214 us (32%)
  starting transfers between devices  198 us (29%)
  Pallas kernels  156 us (23%)
  other arithmetic  64.7 us (10%)
  local copies, waits for them, and re-layouts  33.2 us (5%)
    ppermute x70, starting transfers between devices, exchange(): lax.ppermute(v, 'row', p)  162 us
    ppermute x70, waiting for transfers between devices, exchange(): lax.ppermute(v, 'row', p)  130 us
    pallas_call x8, Pallas kernels, input_kernel(): pl.pallas_call(kernel, grid_spec=pltpu.PrefetchScalarGridSpec(num_scalar_...  49.7 us
    pallas_call x8, Pallas kernels, forward_kernel(): pl.pallas_call(kernel, grid=(wk // TILE,), in_specs=[pl.BlockSpec((rows,...  42.3 us
    pallas_call x8, Pallas kernels, weight_kernel(): pl.pallas_call(kernel, grid_spec=pltpu.PrefetchScalarGridSpec(num_scalar_...  39 us
    ppermute x8, waiting for transfers between devices, run(): wg[k]['x'] = lax.ppermute(keep, 'dp', swap_x)  33.4 us
    unnamed x242, local copies, waits for them, and re-layouts  25.5 us
    pallas_call x8, Pallas kernels, place(): pl.pallas_call(kernel, out_shape=[jax.ShapeDtypeStruct(shape, jnp.float32...  25.1 us
  transfers between devices with their start and end apart: 117, of which 36 were waited for; matrix products, arithmetic and copies ran while one was open for 10% of the time, Pallas kernels for 22%

profile of v3, /device:TPU:0, one launch (start us, length us, event | category | flops | bytes accessed | tf_op | source)
XLA Modules:
  0.0 668.8 jit_solution(10767733696507476339)
XLA Ops:
  5.2 21.9 %collective-permute-done = f32[512,512]{1,0:T(8,128)S(1)} collective-permute-done((f32[512,512]{1,0:T(8,128)}, f32[512,512]{1,0:T(8,128)S(1)}, u32[]{:S(2)}, u32[]{:S(2)}) %collective-permute-start) | collective-permute-done | bytes 1048608 | tf_op jit(solution)/shard_map/ppermute | solution.py:253
  68.1 5.9 collective-permute-done.7
  112.3 6.0 multiply_multiply_fusion.5
  143.2 6.8 %collective-permute-done.12.refs_1_.refs_8_ = f32[128,1024]{1,0:T(8,128)S(1)} collective-permute-done((f32[128,1024]{1,0:T(8,128)S(1)}, f32[128,1024]{1,0:T(8,128)S(1)}, u32[]{:S(2)}, u32[]{:S(2)}) %collective-permute-start.12) | collective-permute-done | bytes 524320 | tf_op jit(solution)/shard_map/ppermute | solution.py:272
  155.1 6.2 collective-permute-done.26.refs_2_.refs_9_
  166.3 6.2 collective-permute-done.14.refs_2_.refs_9_
  205.7 11.6 %collective-permute-done.18 = f32[128,1024]{1,0:T(8,128)S(1)} collective-permute-done((f32[128,1024]{1,0:T(8,128)S(1)}, f32[128,1024]{1,0:T(8,128)S(1)}, u32[]{:S(2)}, u32[]{:S(2)}) %collective-permute-start.18) | collective-permute-done | bytes 524320 | tf_op jit(solution)/shard_map/ppermute | solution.py:272
  228.4 12.2 %collective-permute-start.42 = (f32[128,1024]{1,0:T(8,128)S(1)}, f32[128,1024]{1,0:T(8,128)S(1)}, u32[]{:S(2)}, u32[]{:S(2)}) collective-permute-start(f32[128,1024]{1,0:T(8,128)S(1)} %pad_maximum_fusion.8.refs_0_.refs_7_), channel_id=1, source_target_pairs={{0,2},{6,4},{4,6},{2,0},{1,3},{7,5},{5,7},{3,1},{8,10},{14,12},{12... | collective-permute-start | bytes 1572872 | tf_op jit(solution)/shard_map/ppermute | solution.py:272
  257.5 7.0 %collective-permute-done.34.refs_1_.refs_8_ = f32[128,1024]{1,0:T(8,128)S(1)} collective-permute-done((f32[128,1024]{1,0:T(8,128)S(1)}, f32[128,1024]{1,0:T(8,128)S(1)}, u32[]{:S(2)}, u32[]{:S(2)}) %collective-permute-start.34) | collective-permute-done | bytes 524320 | tf_op jit(solution)/shard_map/ppermute | solution.py:272
  271.4 6.3 shard_map.66.refs_14_
  298.4 6.6 shard_map.67.refs_14_
  335.5 11.5 %collective-permute-done.45 = f32[128,1024]{1,0:T(8,128)S(1)} collective-permute-done((f32[128,1024]{1,0:T(8,128)S(1)}, f32[128,1024]{1,0:T(8,128)S(1)}, u32[]{:S(2)}, u32[]{:S(2)}) %collective-permute-start.45) | collective-permute-done | bytes 524320 | tf_op jit(solution)/shard_map/ppermute | solution.py:272
  355.5 13.5 %collective-permute-start.74 = (f32[128,512]{1,0:T(8,128)S(1)}, f32[128,512]{1,0:T(8,128)S(1)}, u32[]{:S(2)}, u32[]{:S(2)}) collective-permute-start(f32[128,512]{1,0:T(8,128)S(1)} %select_bitcast_fusion.2), channel_id=1, source_target_pairs={{0,2},{6,4},{1,3},{7,5},{8,10},{14,12},{9,11},{15,13},{16,18},{22,... | collective-permute-start | bytes 786440 | tf_op jit(solution)/shard_map/ppermute | solution.py:272
  389.3 7.0 %collective-permute-done.56.refs_1_.refs_8_ = f32[128,1024]{1,0:T(8,128)S(1)} collective-permute-done((f32[128,1024]{1,0:T(8,128)S(1)}, f32[128,1024]{1,0:T(8,128)S(1)}, u32[]{:S(2)}, u32[]{:S(2)}) %collective-permute-start.56) | collective-permute-done | bytes 524320 | tf_op jit(solution)/shard_map/ppermute | solution.py:272
  402.2 6.6 shard_map.72.refs_14_
  415.7 8.7 %collective-permute-done.60.refs_2_ = f32[512,512]{1,0:T(8,128)} collective-permute-done((f32[512,512]{1,0:T(8,128)S(1)}, f32[512,512]{1,0:T(8,128)}, u32[]{:S(2)}, u32[]{:S(2)}) %collective-permute-start.60) | collective-permute-done | bytes 1048608 | tf_op jit(solution)/shard_map/ppermute | solution.py:337
  428.6 6.6 shard_map.73.refs_14_
  504.5 9.8 %collective-permute-start.84 = (f32[128,512]{1,0:T(8,128)S(1)}, f32[128,512]{1,0:T(8,128)S(1)}, u32[]{:S(2)}, u32[]{:S(2)}) collective-permute-start(f32[128,512]{1,0:T(8,128)S(1)} %pad_maximum_fusion.12.refs_0_.refs_7_), channel_id=1, source_target_pairs={{0,2},{6,4},{4,6},{2,0},{1,3},{7,5},{5,7},{3,1},{8,10},{14,12},{12... | collective-permute-start | bytes 786440 | tf_op jit(solution)/shard_map/ppermute | solution.py:272
  533.3 6.5 shard_map.80.refs_14_
  549.6 6.6 shard_map.82.refs_14_
  556.2 14.8 %collective-permute-done.102.refs_3_.refs_10_ = f32[128,1024]{1,0:T(8,128)S(1)} collective-permute-done((f32[128,1024]{1,0:T(8,128)S(1)}, f32[128,1024]{1,0:T(8,128)S(1)}, u32[]{:S(2)}, u32[]{:S(2)}) %collective-permute-start.102) | collective-permute-done | bytes 524320 | tf_op jit(solution)/shard_map/ppermute | solution.py:272
  592.3 6.6 shard_map.84.refs_14_
  598.9 13.3 %collective-permute-done.110.refs_2_ = f32[512,512]{1,0:T(8,128)S(1)} collective-permute-done((f32[512,512]{1,0:T(8,128)S(1)}, f32[512,512]{1,0:T(8,128)S(1)}, u32[]{:S(2)}, u32[]{:S(2)}) %collective-permute-start.110) | collective-permute-done | bytes 1048608 | tf_op jit(solution)/shard_map/ppermute | solution.py:329
  624.5 17.9 %collective-permute-done.106 = f32[2,128,1024]{2,1,0:T(8,128)S(1)} collective-permute-done((f32[2,128,1024]{2,1,0:T(8,128)S(1)}, f32[2,128,1024]{2,1,0:T(8,128)S(1)}, u32[]{:S(2)}, u32[]{:S(2)}) %collective-permute-start.106) | collective-permute-done | bytes 1048608 | tf_op jit(solution)/shard_map/ppermute | solution.py:490
  (589 shorter events, 439.4 us)
Async XLA Ops:
  0.6 26.4 %collective-permute-start = (f32[512,512]{1,0:T(8,128)}, f32[512,512]{1,0:T(8,128)S(1)}, u32[]{:S(2)}, u32[]{:S(2)}) collective-permute-start(f32[512,512]{1,0:T(8,128)} %param.3), channel_id=1, source_target_pairs={{0,1},{1,0},{2,3},{3,2},{4,5},{5,4},{6,7},{7,6},{8,9},{9,8},{10,11... | collective-permute-start | bytes 3145736 | tf_op jit(solution)/shard_map/ppermute | solution.py:253
  3.7 43.0 %collective-permute-start.20 = (f32[512,512]{1,0:T(8,128)}, f32[512,512]{1,0:T(8,128)}, u32[]{:S(2)}, u32[]{:S(2)}) collective-permute-start(f32[512,512]{1,0:T(8,128)} %param.3), channel_id=1, source_target_pairs={{0,16},{16,0},{8,24},{24,8},{1,17},{17,1},{9,25},{25,9},{2,18},{18... | collective-permute-start | bytes 3145736 | tf_op jit(solution)/shard_map/ppermute | solution.py:257
  46.6 32.5 %collective-permute-start.21 = (f32[512,512]{1,0:T(8,128)}, f32[512,512]{1,0:T(8,128)S(1)}, u32[]{:S(2)}, u32[]{:S(2)}) collective-permute-start(f32[512,512]{1,0:T(8,128)} %collective-permute-done.20), channel_id=1, source_target_pairs={{0,1},{1,0},{2,3},{3,2},{4,5},{5,4},{6,7},{7,6},{8,9},{9,8},{10,11... | collective-permute-start | bytes 3145736 | tf_op jit(solution)/shard_map/ppermute | solution.py:253
  75.2 37.1 %collective-permute-start.9 = (f32[128,1024]{1,0:T(8,128)}, f32[128,1024]{1,0:T(8,128)}, u32[]{:S(2)}, u32[]{:S(2)}) collective-permute-start(f32[128,1024]{1,0:T(8,128)} %get-tuple-element.640), channel_id=1, source_target_pairs={{0,2},{6,4},{4,6},{2,0},{1,3},{7,5},{5,7},{3,1},{8,10},{14,12},{12... | collective-permute-start | bytes 1572872 | tf_op jit(solution)/shard_map/ppermute | solution.py:272
  77.7 34.6 %collective-permute-start.10 = (f32[128,1024]{1,0:T(8,128)}, f32[128,1024]{1,0:T(8,128)}, u32[]{:S(2)}, u32[]{:S(2)}) collective-permute-start(f32[128,1024]{1,0:T(8,128)} %get-tuple-element.639), channel_id=1, source_target_pairs={{2,4},{4,2},{3,5},{5,3},{10,12},{12,10},{11,13},{13,11},{18,20},{2... | collective-permute-start | bytes 1572872 | tf_op jit(solution)/shard_map/ppermute | solution.py:272
  86.4 25.9 %collective-permute-start.4 = (f32[128,1024]{1,0:T(8,128)}, f32[128,1024]{1,0:T(8,128)}, u32[]{:S(2)}, u32[]{:S(2)}) collective-permute-start(f32[128,1024]{1,0:T(8,128)} %get-tuple-element.644), channel_id=1, source_target_pairs={{0,2},{6,4},{4,6},{2,0},{1,3},{7,5},{5,7},{3,1},{8,10},{14,12},{12... | collective-permute-start | bytes 1572872 | tf_op jit(solution)/shard_map/ppermute | solution.py:272
  252.8 24.9 %collective-permute-start.48 = (f32[128,1024]{1,0:T(8,128)S(1)}, f32[128,1024]{1,0:T(8,128)S(1)}, u32[]{:S(2)}, u32[]{:S(2)}) collective-permute-start(f32[128,1024]{1,0:T(8,128)S(1)} %broadcast_select_fusion.16), channel_id=1, source_target_pairs={{0,2},{6,4},{4,6},{2,0},{1,3},{7,5},{5,7},{3,1},{8,10},{14,12},{12... | collective-permute-start | bytes 1572872 | tf_op jit(solution)/shard_map/ppermute | solution.py:272
  278.2 26.9 %collective-permute-start.50 = (f32[128,1024]{1,0:T(8,128)S(1)}, f32[128,1024]{1,0:T(8,128)S(1)}, u32[]{:S(2)}, u32[]{:S(2)}) collective-permute-start(f32[128,1024]{1,0:T(8,128)S(1)} %broadcast_select_fusion.14), channel_id=1, source_target_pairs={{0,2},{6,4},{4,6},{2,0},{1,3},{7,5},{5,7},{3,1},{8,10},{14,12},{12... | collective-permute-start | bytes 1572872 | tf_op jit(solution)/shard_map/ppermute | solution.py:272
  280.8 24.3 %collective-permute-start.51 = (f32[128,1024]{1,0:T(8,128)S(1)}, f32[128,1024]{1,0:T(8,128)S(1)}, u32[]{:S(2)}, u32[]{:S(2)}) collective-permute-start(f32[128,1024]{1,0:T(8,128)S(1)} %get-tuple-element.585), channel_id=1, source_target_pairs={{2,4},{4,2},{3,5},{5,3},{10,12},{12,10},{11,13},{13,11},{18,20},{2... | collective-permute-start | bytes 1572872 | tf_op jit(solution)/shard_map/ppermute | solution.py:272
  306.2 28.6 %collective-permute-start.52 = (f32[128,1024]{1,0:T(8,128)}, f32[128,1024]{1,0:T(8,128)}, u32[]{:S(2)}, u32[]{:S(2)}) collective-permute-start(f32[128,1024]{1,0:T(8,128)} %get-tuple-element.632), channel_id=1, source_target_pairs={{0,2},{6,4},{4,6},{2,0},{1,3},{7,5},{5,7},{3,1},{8,10},{14,12},{12... | collective-permute-start | bytes 1572872 | tf_op jit(solution)/shard_map/ppermute | solution.py:272
  355.5 45.5 %collective-permute-start.74 = (f32[128,512]{1,0:T(8,128)S(1)}, f32[128,512]{1,0:T(8,128)S(1)}, u32[]{:S(2)}, u32[]{:S(2)}) collective-permute-start(f32[128,512]{1,0:T(8,128)S(1)} %select_bitcast_fusion.2), channel_id=1, source_target_pairs={{0,2},{6,4},{1,3},{7,5},{8,10},{14,12},{9,11},{15,13},{16,18},{22,... | collective-permute-start | bytes 786440 | tf_op jit(solution)/shard_map/ppermute | solution.py:272
  371.6 24.6 %collective-permute-start.56 = (f32[128,1024]{1,0:T(8,128)S(1)}, f32[128,1024]{1,0:T(8,128)S(1)}, u32[]{:S(2)}, u32[]{:S(2)}) collective-permute-start(f32[128,1024]{1,0:T(8,128)S(1)} %pad_maximum_fusion.9.refs_0_.refs_7_), channel_id=1, source_target_pairs={{0,2},{6,4},{4,6},{2,0},{1,3},{7,5},{5,7},{3,1},{8,10},{14,12},{12... | collective-permute-start | bytes 1572872 | tf_op jit(solution)/shard_map/ppermute | solution.py:272
  408.9 49.5 %collective-permute-start.69 = (f32[512,512]{1,0:T(8,128)}, f32[512,512]{1,0:T(8,128)}, u32[]{:S(2)}, u32[]{:S(2)}) collective-permute-start(f32[512,512]{1,0:T(8,128)} %add.471.refs_0_), channel_id=1, source_target_pairs={{0,8},{8,0},{16,24},{24,16},{1,9},{9,1},{17,25},{25,17},{2,10},{10... | collective-permute-start | bytes 3145736 | tf_op jit(solution)/shard_map/ppermute | solution.py:330
  409.0 53.9 %collective-permute-start.70 = (f32[512,512]{1,0:T(8,128)S(1)}, f32[512,512]{1,0:T(8,128)}, u32[]{:S(2)}, u32[]{:S(2)}) collective-permute-start(f32[512,512]{1,0:T(8,128)S(1)} %copy-done.102), channel_id=1, source_target_pairs={{0,8},{8,0},{16,24},{24,16},{1,9},{9,1},{17,25},{25,17},{2,10},{10... | collective-permute-start | bytes 3145736 | tf_op jit(solution)/shard_map/ppermute | solution.py:345
  495.7 30.4 %collective-permute-start.87 = (f32[512,512]{1,0:T(8,128)S(1)}, f32[512,512]{1,0:T(8,128)S(1)}, u32[]{:S(2)}, u32[]{:S(2)}) collective-permute-start(f32[512,512]{1,0:T(8,128)S(1)} %copy-done.86), channel_id=1, source_target_pairs={{0,8},{8,0},{16,24},{24,16},{1,9},{9,1},{17,25},{25,17},{2,10},{10... | collective-permute-start | bytes 3145736 | tf_op jit(solution)/shard_map/ppermute | solution.py:345
  503.3 26.5 %collective-permute-start.98 = (f32[512,512]{1,0:T(8,128)S(1)}, f32[512,512]{1,0:T(8,128)}, u32[]{:S(2)}, u32[]{:S(2)}) collective-permute-start(f32[512,512]{1,0:T(8,128)S(1)} %add.515.refs_0_), channel_id=1, source_target_pairs={{0,16},{16,0},{8,24},{24,8},{1,17},{17,1},{9,25},{25,9},{2,18},{18... | collective-permute-start | bytes 3145736 | tf_op jit(solution)/shard_map/ppermute | solution.py:337
  532.4 38.7 %collective-permute-start.101 = (f32[512,512]{1,0:T(8,128)S(1)}, f32[512,512]{1,0:T(8,128)}, u32[]{:S(2)}, u32[]{:S(2)}) collective-permute-start(f32[512,512]{1,0:T(8,128)S(1)} %add.513.refs_0_), channel_id=1, source_target_pairs={{0,16},{16,0},{8,24},{24,8},{1,17},{17,1},{9,25},{25,9},{2,18},{18... | collective-permute-start | bytes 3145736 | tf_op jit(solution)/shard_map/ppermute | solution.py:337
  548.2 34.2 %collective-permute-start.100 = (f32[512,512]{1,0:T(8,128)S(1)}, f32[512,512]{1,0:T(8,128)S(1)}, u32[]{:S(2)}, u32[]{:S(2)}) collective-permute-start(f32[512,512]{1,0:T(8,128)S(1)} %add.513.refs_0_), channel_id=1, source_target_pairs={{0,8},{8,0},{16,24},{24,16},{1,9},{9,1},{17,25},{25,17},{2,10},{10... | collective-permute-start | bytes 3145736 | tf_op jit(solution)/shard_map/ppermute | solution.py:330
  587.9 24.3 %collective-permute-start.110 = (f32[512,512]{1,0:T(8,128)S(1)}, f32[512,512]{1,0:T(8,128)S(1)}, u32[]{:S(2)}, u32[]{:S(2)}) collective-permute-start(f32[512,512]{1,0:T(8,128)S(1)} %add.520.refs_0_), channel_id=1, source_target_pairs={{0,16},{16,0},{8,24},{24,8},{1,17},{17,1},{9,25},{25,9},{2,18},{18... | collective-permute-start | bytes 3145736 | tf_op jit(solution)/shard_map/ppermute | solution.py:329
  616.2 26.2 %collective-permute-start.106 = (f32[2,128,1024]{2,1,0:T(8,128)S(1)}, f32[2,128,1024]{2,1,0:T(8,128)S(1)}, u32[]{:S(2)}, u32[]{:S(2)}) collective-permute-start(f32[2,128,1024]{2,1,0:T(8,128)S(1)} %slice_bitcast_fusion), channel_id=1, source_target_pairs={{0,16},{16,0},{8,24},{24,8},{1,17},{17,1},{9,25},{25,9},{2,18},{18... | collective-permute-start | bytes 3145736 | tf_op jit(solution)/shard_map/ppermute | solution.py:490
  619.3 25.5 %collective-permute-start.108 = (f32[2,2,128,512]{3,2,1,0:T(8,128)S(1)}, f32[2,2,128,512]{3,2,1,0:T(8,128)S(1)}, u32[]{:S(2)}, u32[]{:S(2)}) collective-permute-start(f32[2,2,128,512]{3,2,1,0:T(8,128)S(1)} %slice_select_fusion), channel_id=1, source_target_pairs={{0,1},{1,0},{2,3},{3,2},{4,5},{5,4},{6,7},{7,6},{8,9},{9,8},{10,11... | collective-permute-start | bytes 3145736 | tf_op jit(solution)/shard_map/ppermute | solution.py:497
  622.7 28.9 %collective-permute-start.113 = (f32[512,512]{1,0:T(8,128)S(1)}, f32[512,512]{1,0:T(8,128)S(1)}, u32[]{:S(2)}, u32[]{:S(2)}) collective-permute-start(f32[512,512]{1,0:T(8,128)S(1)} %add.520.refs_0_), channel_id=1, source_target_pairs={{0,8},{8,0},{16,24},{24,16},{1,9},{9,1},{17,25},{25,17},{2,10},{10... | collective-permute-start | bytes 3145736 | tf_op jit(solution)/shard_map/ppermute | solution.py:330
  622.7 30.9 %collective-permute-start.114 = (f32[512,512]{1,0:T(8,128)S(1)}, f32[512,512]{1,0:T(8,128)S(1)}, u32[]{:S(2)}, u32[]{:S(2)}) collective-permute-start(f32[512,512]{1,0:T(8,128)S(1)} %collective-permute-done.110.refs_2_), channel_id=1, source_target_pairs={{0,8},{8,0},{16,24},{24,16},{1,9},{9,1},{17,25},{25,17},{2,10},{10... | collective-permute-start | bytes 3145736 | tf_op jit(solution)/shard_map/ppermute | solution.py:345
  623.3 30.3 %collective-permute-start.115 = (f32[512,256]{1,0:T(8,128)S(1)}, f32[512,256]{1,0:T(8,128)S(1)}, u32[]{:S(2)}, u32[]{:S(2)}) collective-permute-start(f32[512,256]{1,0:T(8,128)S(1)} %add.521.refs_0_), channel_id=1, source_target_pairs={{0,16},{16,0},{8,24},{24,8},{1,17},{17,1},{9,25},{25,9},{2,18},{18... | collective-permute-start | bytes 1572872 | tf_op jit(solution)/shard_map/ppermute | solution.py:329
  (213 other events, 3618.5 us)
